TPU v7x, 256 devices: a whole 4x4x8 slice. The times are simulated.
256 devices in a mesh: node: 32 (over z_hi, y, x), local: 8 (over z_lo, core).
Axes of the slice: x: 4, y: 4, z: 8 (z_hi: 2, z_lo: 4; z = z_hi * 4 + z_lo), core: 2. Of those that a mesh axis runs over, the one named last changes fastest.
Arguments:
- tokens: bfloat16 [131072, 4096], P(('node', 'local')), may hold values from -24 to 24
- out_grad: bfloat16 [131072, 1024], P(('node', 'local')), may hold values from -8.9375 to 8.9375
- next_tokens: bfloat16 [131072, 4096], P(('node', 'local')), may hold values from -6 to 6
- overflow: int32 [256], P(('node', 'local')), may hold values from 0 to 1, as said below
- master: float32 [4096, 1024], P(('node', 'local')), may hold values from -0.09375 to 0.09375
- first_moment: float32 [4096, 1024], P(('node', 'local')), may hold values from -12 to 12
- second_moment: float32 [4096, 1024], P(('node', 'local')), may hold values from 1 to 16
Outputs:
- new_master: float32 [4096, 1024], P(('node', 'local'))
- new_first: float32 [4096, 1024], P(('node', 'local'))
- new_second: float32 [4096, 1024], P(('node', 'local'))
- secondary: bfloat16 [32, 128, 1024], P(None, 'local')
- next_projection: bfloat16 [131072, 1024], P(('node', 'local'))
Inputs may be any that keep to these rules, and one draw needn't show every extreme that they name: At least one device has overflow 0 and at least one has overflow 1.
All inputs are finite; a program needn't handle non-finite values.
Results may differ from a plain program's by a relative error of at most 0.0049.
Values may be sent and summed in bfloat16 or wider, within the bound.
A program may use at most 128 MiB of HBM per device.

v0:
```python
import jax
import jax.numpy as jnp
from jax import lax
from jax.sharding import PartitionSpec as P

STEP = 10


def body(tokens, out_grad, next_tokens, overflow, master, first_moment, second_moment):
    nodes = lax.axis_size("node")
    locals_count = lax.axis_size("local")
    shard_rows = master.shape[0]
    tok_rows = tokens.shape[0]
    kept_scale = (1 - overflow[0]).astype(jnp.float32)
    count = lax.psum(kept_scale, ("node", "local"))
    columns = tokens
    summed = lax.psum_scatter(
        kept_scale * jnp.einsum("tr,tk->rk", columns, out_grad, preferred_element_type=jnp.float32),
        ("node", "local"),
        scatter_dimension=0,
        tiled=True,
    )
    grad = summed / count
    new_first = 0.9 * first_moment + 0.1 * grad
    new_second = 0.95 * second_moment + 0.05 * grad * grad
    update = new_first / (1.0 - 0.9**STEP) / (jnp.sqrt(new_second / (1.0 - 0.95**STEP)) + 1e-08)
    new_master = master - 0.001 * (update + 0.1 * master)
    weights = new_master.astype(jnp.bfloat16)
    secondary = lax.all_gather(weights[None], "node", axis=0, tiled=True)
    next_grouped = next_tokens.reshape(tok_rows, nodes, locals_count, shard_rows)
    columns = next_grouped
    projected = jnp.einsum(
        "tnlr,nlrk->tk",
        columns,
        lax.all_gather(secondary[:, None], "local", axis=1, tiled=True),
        preferred_element_type=jnp.float32,
    )
    next_projection = projected.astype(jnp.bfloat16)
    return (new_master, new_first, new_second, secondary, next_projection)


def solution(mesh):
    return jax.shard_map(
        body,
        mesh=mesh,
        in_specs=(
            P(("node", "local"), None),
            P(("node", "local"), None),
            P(("node", "local"), None),
            P(("node", "local")),
            P(("node", "local"), None),
            P(("node", "local"), None),
            P(("node", "local"), None),
        ),
        out_specs=(
            P(("node", "local"), None),
            P(("node", "local"), None),
            P(("node", "local"), None),
            P(None, "local", None),
            P(("node", "local"), None),
        ),
        check_vma=False,
    )
```

profile of v0, /device:TPU:1, one launch (start us, length us, event | category | flops | bytes accessed | tf_op | source)
XLA Modules:
  0.0 1516.1 jit_solution(599585477485905912)
XLA Ops:
  7.2 0.0 copy-start
  7.2 0.0 reduce-scatter.2.cloned.1.call-start
  8.0 0.5 copy-done
  8.4 10.3 broadcast_multiply_fusion
  18.8 0.0 copy-start.3
  18.8 0.0 copy-start.4
  18.8 0.0 copy-start.5
  18.8 0.0 reduce-scatter.2.cloned.1.call-update
  18.8 0.0 all-gather.5.cloned.1.call-start
  18.8 82.8 %psum.7 = f32[]{:T(128)} all-reduce(f32[]{:T(128)} %bitcast), channel_id=1, replica_groups=mesh['node'=32,'local'=8] {'node','local'}, use_global_device_ids=true, to_apply=%region_1.0 | all-reduce | flops 1 | bytes 8 | tf_op jit(solution)/shard_map/psum | solution.py:15
  101.6 1211.5 %reduce-scatter.2.cloned.1.call-done = f32[16,1024]{1,0:T(8,128)} async-done(((f32[4096,1024]{1,0:T(8,128)}), f32[16,1024]{1,0:T(8,128)}) %reduce-scatter.2.cloned.1.call-update) | async-done | bytes 65552 | tf_op jit(solution)/shard_map/reduce_scatter | solution.py:17
  1313.1 0.0 copy-done.3
  1313.1 0.0 copy-done.4
  1313.1 0.0 copy-done.5
  1313.1 2.2 fusion.8
  1315.3 0.0 all-gather.5.cloned.1.call-update
  1315.3 0.0 all-gather.7.cloned.1.call-start
  1315.4 81.8 %all-gather.5.cloned.1.call-done = bf16[512,1024]{1,0:T(8,128)(2,1)} async-done(((bf16[16,1024]{1,0:T(8,128)(2,1)}), bf16[512,1024]{1,0:T(8,128)(2,1)}) %all-gather.5.cloned.1.call-update) | async-done | bytes 1048592 | tf_op jit(solution)/shard_map/all_gather | solution.py:29
  1397.2 0.0 all-gather.7.cloned.1.call-update
  1397.2 6.5 copy.16
  1403.7 82.8 %all-gather.7.cloned.1.call-done = bf16[32,128,1024]{2,1,0:T(8,128)(2,1)} async-done(((bf16[32,16,1024]{2,1,0:T(8,128)(2,1)}), bf16[32,128,1024]{2,1,0:T(8,128)(2,1)}) %all-gather.7.cloned.1.call-update) | async-done | bytes 8388624 | tf_op jit(solution)/shard_map/all_gather | solution.py:35
  1486.4 0.0 copy-start.1
  1486.4 11.5 copy.15
  1497.9 0.0 copy-done.1
  1497.9 0.0 copy-start.2
  1497.9 8.4 fusion.4
  1506.3 2.3 copy.18
  1508.6 0.0 copy-done.2
  1508.6 1.0 copy.28
Async XLA Ops:
  7.2 1.2 copy-start
  7.2 1305.9 %reduce-scatter.2.cloned.1.call-start = ((), (), s32[]{:S(2)}) async-start(), calls=%async_computation.1 | async-start | bytes 16842752 | tf_op jit(solution)/shard_map/reduce_scatter | solution.py:17
  18.8 1294.3 %copy-start.3 = (f32[16,1024]{1,0:T(8,128)S(1)}, f32[16,1024]{1,0:T(8,128)}, u32[]{:S(2)}) copy-start(f32[16,1024]{1,0:T(8,128)} %param.11) | copy-start | bytes 196612
  18.8 1294.3 %copy-start.4 = (f32[16,1024]{1,0:T(8,128)S(1)}, f32[16,1024]{1,0:T(8,128)}, u32[]{:S(2)}) copy-start(f32[16,1024]{1,0:T(8,128)} %param.12) | copy-start | bytes 196612
  18.8 1294.3 %copy-start.5 = (f32[16,1024]{1,0:T(8,128)S(1)}, f32[16,1024]{1,0:T(8,128)}, u32[]{:S(2)}) copy-start(f32[16,1024]{1,0:T(8,128)} %param.13) | copy-start | bytes 196612
  18.8 1378.4 %all-gather.5.cloned.1.call-start = ((), (), s32[]{:S(2)}) async-start(), calls=%async_computation.2 | async-start | bytes 1081344 | tf_op jit(solution)/shard_map/all_gather | solution.py:29
  1315.3 171.1 %all-gather.7.cloned.1.call-start = ((), (), s32[]{:S(2)}) async-start(), calls=%async_computation.3 | async-start | bytes 9437184 | tf_op jit(solution)/shard_map/all_gather | solution.py:35
  1486.4 11.5 copy-start.1
  1497.9 10.7 copy-start.2
Sparse Core Ops, SparseCore 0:
  18.9 1294.1 reduce-scatter.1
  1317.6 79.4 all-gather.4
  1399.1 87.3 all-gather.6
where the time goes:
time: 1520 us
  waiting for transfers between devices  1380 us (91%)
  blocking collectives  82.8 us (5%)
  local copies, waits for them, and re-layouts  21.7 us (1%)
  matrix products  18.8 us (1%)
    reduce_scatter x1, waiting for transfers between devices, body(): lax.psum_scatter(kept_scale * jnp.einsum('tr,tk->rk', columns, out_grad,...  1210 us
    psum x1, blocking collectives, body(): count = lax.psum(kept_scale, ('node', 'local'))  82.8 us
    all_gather x1, waiting for transfers between devices, body(): lax.all_gather(secondary[:, None], 'local', axis=1, tiled=True)  82.8 us
    all_gather x1, waiting for transfers between devices, body(): secondary = lax.all_gather(weights[None], 'node', axis=0, tiled=True)  81.8 us
  transfers between devices with their start and end apart: 3, of which 3 were waited for; matrix products, arithmetic and copies ran while one was open for 0% of the time, Pallas kernels for 0%

commit v1 on v0

v1 whole, which is shorter than its diff:
```python
import functools

import jax
import jax.numpy as jnp
from jax import lax
from jax.experimental import pallas as pl
from jax.experimental.pallas import tpu as pltpu
from jax.sharding import PartitionSpec as P

STEP = 10
MESH = pl.DeviceIdType.MESH
NH, NY, NX, NL, NC = 2, 4, 4, 4, 2
NZ = NH * NL
F32, BF16 = jnp.float32, jnp.bfloat16


def kernel(
    ov, tok_hbm, og_hbm, nxt_hbm, master, first, second,
    o_master, o_first, o_second, o_sec, o_proj,
    tok, og, nxt, own, sib_out, sib_in, s1,
    r1x, r1y, r1z, s2x, s2y, s2z, r2x, r2y, r2z, s3a, s3z, r3a, r3z,
    cnt, cnt_in, w, acc,
    in_sem, tok_sem, out_sem, sib_send, sib_recv, cnt_send, cnt_recv,
    p1_send, p1x_recv, p1y_recv, p1z_recv,
    p2_send, p2x_recv, p2y_recv, p2z_recv, p3_send, p3a_recv, p3z_recv,
    a3_send, a3a_recv, a3z_recv, a2_send, a2x_recv, a2y_recv, a2z_recv,
    a1_send, a1x_recv, a1y_recv, a1z_recv, f_send, fx_recv, fy_recv, fz_recv,
):
    rows, kv = master.shape
    ca, cb = r1x.shape[-1], r1x.shape[-1] + r1y.shape[-1]
    colx, coly, colz, colxy = pl.ds(0, ca), pl.ds(ca, cb - ca), pl.ds(cb, kv - cb), pl.ds(0, cb)
    node, loc = lax.axis_index("node"), lax.axis_index("local")
    x, y, h = lax.rem(node, NX), lax.rem(lax.div(node, NX), NY), lax.div(node, NX * NY)
    c, l = lax.rem(loc, NC), lax.div(loc, NC)

    def dev(hh=h, yy=y, xx=x, ll=l, cc=c):
        return ((hh * NY + yy) * NX + xx, ll * NC + cc)

    def xs(d):
        return lax.rem(x + d, NX)

    def ys(d):
        return lax.rem(y + d, NY)

    def hs(e):
        return lax.rem(h + e, NH)

    def ls(f):
        return lax.rem(l + f, NL)

    xd, yd = range(1, NX), range(1, NY)
    zd = [(e, f) for e in range(NH) for f in range(NL)][1:]
    sib = dev(cc=1 - c)

    def remote(src, dst, send, recv, to):
        return pltpu.make_async_remote_copy(
            src_ref=src, dst_ref=dst, send_sem=send, recv_sem=recv, device_id=to, device_id_type=MESH
        )

    def wait_recv(ref, sem):
        remote(ref, ref, sem, sem, sib).wait_recv()

    def wait_send(ref, sem):
        remote(ref, ref, sem, sem, sib).wait_send()

    og_copy = pltpu.make_async_copy(og_hbm, og, in_sem.at[0])
    nxt_copy = pltpu.make_async_copy(nxt_hbm, nxt, in_sem.at[1])
    og_copy.start()
    width = NX * NL * NC * rows
    steps = NH * NY

    def place(it):
        e, d = lax.rem(it, NH), lax.rem(lax.div(it, NH) + 1, NY)
        return e, d, hs(e), ys(d)

    def tok_copy(it):
        _, _, hh, yy = place(it)
        cols = pl.ds(pl.multiple_of((hh * NY + yy) * width, width), width)
        return pltpu.make_async_copy(tok_hbm.at[:, cols], tok.at[it], tok_sem.at[it])

    @pl.loop(0, steps)
    def _(it):
        tok_copy(it).start()

    nxt_copy.start()
    peers = [sib]
    peers += [dev(xx=xs(d)) for d in xd] + [dev(yy=ys(d)) for d in yd]
    peers += [dev(hh=hs(e), ll=ls(f)) for e, f in zd]
    barrier = pltpu.get_barrier_semaphore()
    for to in peers:
        pl.semaphore_signal(barrier, inc=1, device_id=to, device_id_type=MESH)
    kept = (1 - ov[0]).astype(F32)
    cnt[0] = jnp.full(cnt.shape[1:], kept, F32)
    og_copy.wait()
    og[...] = og[...] * kept.astype(BF16)
    pl.semaphore_wait(barrier, len(peers))
    remote(cnt.at[0], cnt_in.at[0], cnt_send.at[0], cnt_recv.at[0], sib).start()

    def exchange_first(it):
        e, d, hh, yy = place(it)
        wait_recv(sib_in.at[hh, yy], sib_recv.at[it])
        s1[hh, yy] = (own[hh, yy] + sib_in[hh, yy].astype(F32)).astype(BF16)
        for k in xd:
            remote(
                s1.at[hh, yy, xs(k), :, :, colx], r1x.at[k - 1, hh, yy],
                p1_send.at[0], p1x_recv.at[k - 1], dev(xx=xs(k)),
            ).start()

        @pl.when(d > 0)
        def _():
            remote(
                s1.at[hh, yy, :, :, :, coly], r1y.at[d - 1, hh],
                p1_send.at[1], p1y_recv.at[d - 1], dev(yy=yy),
            ).start()

        def send_z(f):
            ll = ls(f)
            slot = e * NL + f - 1
            remote(
                s1.at[hh, yy, :, ll, :, colz], r1z.at[slot, yy],
                p1_send.at[2], p1z_recv.at[slot], dev(hh=hh, ll=ll),
            ).start()

        for f in range(1, NL):
            send_z(f)

        @pl.when(e > 0)
        def _():
            send_z(0)

    @pl.loop(0, steps)
    def _(it):
        _, _, hh, yy = place(it)
        tok_copy(it).wait()
        part = lax.dot_general(tok[it], og[...], (((0,), (0,)), ((), ())), preferred_element_type=F32)
        part = part.reshape(NX, NL, NC, rows, kv)
        even, odd = part[:, :, 0], part[:, :, 1]
        own[hh, yy] = jnp.where(c == 0, even, odd)
        sib_out[hh, yy] = jnp.where(c == 0, odd, even).astype(BF16)
        remote(sib_out.at[hh, yy], sib_in.at[hh, yy], sib_send.at[0], sib_recv.at[it], sib).start()

        @pl.when(it > 0)
        def _():
            exchange_first(it - 1)

    exchange_first(jnp.int32(steps - 1))

    wait_recv(cnt_in.at[0], cnt_recv.at[0])
    cnt[1] = cnt[0] + cnt_in[0]
    for k in xd:
        remote(cnt.at[1], cnt_in.at[k], cnt_send.at[1], cnt_recv.at[k], dev(xx=xs(k))).start()

    for k in xd:
        wait_recv(r1x.at[k - 1], p1x_recv.at[k - 1])

    @pl.loop(0, NH * NY)
    def _(i):
        hh, yy = lax.div(i, NY), lax.rem(i, NY)
        total = s1[hh, yy, x, :, :, colx].astype(F32)
        for k in xd:
            total += r1x[k - 1, hh, yy].astype(F32)
        s2x[hh, yy] = total.astype(BF16)

    for k in yd:
        remote(s2x.at[:, ys(k)], r2x.at[k - 1], p2_send.at[0], p2x_recv.at[k - 1], dev(yy=ys(k))).start()

    for k in yd:
        wait_recv(r1y.at[k - 1], p1y_recv.at[k - 1])

    @pl.loop(0, NH * NX)
    def _(i):
        hh, xx = lax.div(i, NX), lax.rem(i, NX)
        total = s1[hh, y, xx, :, :, coly].astype(F32)
        for k in yd:
            total += r1y[k - 1, hh, xx].astype(F32)
        s2y[hh, xx] = total.astype(BF16)

    for k in xd:
        remote(s2y.at[:, xs(k)], r2y.at[k - 1], p2_send.at[1], p2y_recv.at[k - 1], dev(xx=xs(k))).start()

    for k in range(1, NZ):
        wait_recv(r1z.at[k - 1], p1z_recv.at[k - 1])

    @pl.loop(0, NY)
    def _(yy):
        total = s1[h, yy, :, l, :, colz].astype(F32)
        for k in range(1, NZ):
            total += r1z[k - 1, yy].astype(F32)
        s2z[yy] = total.astype(BF16)

    for k in xd:
        remote(s2z.at[:, xs(k)], r2z.at[k - 1], p2_send.at[2], p2z_recv.at[k - 1], dev(xx=xs(k))).start()

    for k in xd:
        wait_recv(cnt_in.at[k], cnt_recv.at[k])
    cnt[2] = cnt[1] + cnt_in[1] + cnt_in[2] + cnt_in[3]
    for k in yd:
        remote(cnt.at[2], cnt_in.at[NX - 1 + k], cnt_send.at[2], cnt_recv.at[NX - 1 + k], dev(yy=ys(k))).start()

    for k in yd:
        wait_recv(r2x.at[k - 1], p2x_recv.at[k - 1])
    total = s2x[:, y].astype(F32)
    for k in yd:
        total += r2x[k - 1].astype(F32)
    s3a[:, :, :, colx] = total.astype(BF16)
    for k in xd:
        wait_recv(r2y.at[k - 1], p2y_recv.at[k - 1])
    total = s2y[:, x].astype(F32)
    for k in xd:
        total += r2y[k - 1].astype(F32)
    s3a[:, :, :, coly] = total.astype(BF16)
    for e, f in zd:
        slot = e * NL + f - 1
        remote(
            s3a.at[hs(e), ls(f)], r3a.at[slot], p3_send.at[0], p3a_recv.at[slot], dev(hh=hs(e), ll=ls(f))
        ).start()
    for k in xd:
        wait_recv(r2z.at[k - 1], p2z_recv.at[k - 1])
    total = s2z[:, x].astype(F32)
    for k in xd:
        total += r2z[k - 1].astype(F32)
    s3z[...] = total.astype(BF16)
    for k in yd:
        remote(s3z.at[ys(k)], r3z.at[k - 1], p3_send.at[1], p3z_recv.at[k - 1], dev(yy=ys(k))).start()

    base = NX + NY - 1
    for k in yd:
        wait_recv(cnt_in.at[NX - 1 + k], cnt_recv.at[NX - 1 + k])
    cnt[3] = cnt[2] + cnt_in[NX] + cnt_in[NX + 1] + cnt_in[NX + 2]
    for e, f in zd:
        slot = base + e * NL + f - 1
        remote(cnt.at[3], cnt_in.at[slot], cnt_send.at[3], cnt_recv.at[slot], dev(hh=hs(e), ll=ls(f))).start()

    for k in range(1, NZ):
        wait_recv(r3a.at[k - 1], p3a_recv.at[k - 1])
    sum_a = s3a[h, l].astype(F32)
    for k in range(1, NZ):
        sum_a += r3a[k - 1].astype(F32)
    for k in yd:
        wait_recv(r3z.at[k - 1], p3z_recv.at[k - 1])
    sum_z = s3z[y].astype(F32)
    for k in yd:
        sum_z += r3z[k - 1].astype(F32)
    for k in range(1, NZ):
        wait_recv(cnt_in.at[base + k - 1], cnt_recv.at[base + k - 1])
    count = cnt[3]
    for k in range(1, NZ):
        count += cnt_in[base + k - 1]
    count = count[0:1, 0:1]

    def adam(cols, summed):
        grad = summed / count
        new_first = 0.9 * first[:, cols] + 0.1 * grad
        new_second = 0.95 * second[:, cols] + 0.05 * grad * grad
        update = new_first / (1.0 - 0.9**STEP) / (jnp.sqrt(new_second / (1.0 - 0.95**STEP)) + 1e-08)
        new_master = master[:, cols] - 0.001 * (update + 0.1 * master[:, cols])
        o_first[:, cols] = new_first
        o_second[:, cols] = new_second
        o_master[:, cols] = new_master
        w[h, y, x, l, c, :, cols] = new_master.astype(BF16)

    adam(colxy, sum_a)
    adam(colz, sum_z)

    def gather(ref, send, recv, to):
        remote(ref, ref, send, recv, to).start()

    for e, f in zd:
        gather(w.at[h, y, x, l, c, :, colxy], a3_send.at[0], a3a_recv.at[e * NL + f - 1], dev(hh=hs(e), ll=ls(f)))
    for k in yd:
        gather(w.at[h, y, x, l, c, :, colz], a3_send.at[1], a3z_recv.at[k - 1], dev(yy=ys(k)))
    for k in range(1, NZ):
        wait_recv(r3a.at[k - 1], a3a_recv.at[k - 1])
    for k in yd:
        gather(w.at[:, y, x, :, c, :, colx], a2_send.at[0], a2x_recv.at[k - 1], dev(yy=ys(k)))
    for k in xd:
        gather(w.at[:, y, x, :, c, :, coly], a2_send.at[1], a2y_recv.at[k - 1], dev(xx=xs(k)))
    for k in yd:
        wait_recv(r3z.at[k - 1], a3z_recv.at[k - 1])
    for k in xd:
        gather(w.at[h, :, x, l, c, :, colz], a2_send.at[2], a2z_recv.at[k - 1], dev(xx=xs(k)))

    for k in yd:
        wait_recv(r2x.at[k - 1], a2x_recv.at[k - 1])
    for k in xd:
        gather(w.at[:, :, x, :, c, :, colx], a1_send.at[0], a1x_recv.at[k - 1], dev(xx=xs(k)))
    for k in xd:
        wait_recv(r2y.at[k - 1], a2y_recv.at[k - 1])
    for k in yd:
        gather(w.at[:, y, :, :, c, :, coly], a1_send.at[1], a1y_recv.at[k - 1], dev(yy=ys(k)))
    for k in xd:
        wait_recv(r2z.at[k - 1], a2z_recv.at[k - 1])
    for e, f in zd:
        gather(w.at[h, :, :, l, c, :, colz], a1_send.at[2], a1z_recv.at[e * NL + f - 1], dev(hh=hs(e), ll=ls(f)))

    gather(w.at[:, :, x, :, c, :, colx], f_send.at[0], fx_recv.at[0], sib)
    gather(w.at[:, y, :, :, c, :, coly], f_send.at[1], fy_recv.at[0], sib)
    gather(w.at[h, :, :, l, c, :, colz], f_send.at[2], fz_recv.at[0], sib)
    for k in xd:
        wait_recv(r1x.at[k - 1], a1x_recv.at[k - 1])
        gather(w.at[:, :, xs(NX - k), :, c, :, colx], f_send.at[0], fx_recv.at[k], sib)
    for k in yd:
        wait_recv(r1y.at[k - 1], a1y_recv.at[k - 1])
        gather(w.at[:, ys(NY - k), :, :, c, :, coly], f_send.at[1], fy_recv.at[k], sib)
    for e, f in zd:
        slot = e * NL + f - 1
        wait_recv(r1z.at[slot], a1z_recv.at[slot])
        gather(w.at[hs(NH - e), :, :, ls(NL - f), c, :, colz], f_send.at[2], fz_recv.at[slot + 1], sib)

    sec_copy = pltpu.make_async_copy(w.at[:, :, :, l, c], o_sec, out_sem.at[0])
    sec_copy.start()

    nxt_copy.wait()
    for k in range(NX):
        wait_recv(r1x.at[0], fx_recv.at[k])
    for k in range(NY):
        wait_recv(r1y.at[0], fy_recv.at[k])
    for k in range(NZ):
        wait_recv(r1z.at[0], fz_recv.at[k])

    acc[...] = jnp.zeros_like(acc)

    @pl.loop(0, steps)
    def _(i):
        hh, yy = lax.div(i, NY), lax.rem(i, NY)
        cols = pl.ds(pl.multiple_of(i * width, width), width)
        acc[...] += jnp.dot(nxt[:, cols], w[hh, yy].reshape(width, kv), preferred_element_type=F32)

    o_proj[...] = acc[...].astype(BF16)
    sec_copy.wait()

    wait_send(sib_out, sib_send.at[0])
    wait_send(cnt.at[0], cnt_send.at[0])
    wait_send(cnt_in.at[pl.ds(0, NX - 1)], cnt_send.at[1])
    wait_send(cnt_in.at[pl.ds(0, NY - 1)], cnt_send.at[2])
    wait_send(cnt_in.at[pl.ds(0, NZ - 1)], cnt_send.at[3])
    for i, ref in enumerate((r1x, r1y, r1z)):
        wait_send(ref, p1_send.at[i])
        wait_send(ref, a1_send.at[i])
    for i, ref in enumerate((r2x, r2y, r2z)):
        wait_send(ref, p2_send.at[i])
        wait_send(ref, a2_send.at[i])
    for i, ref in enumerate((r3a, r3z)):
        wait_send(ref, p3_send.at[i])
        wait_send(ref, a3_send.at[i])
    for i, cols in enumerate((colx, coly, colz)):
        wait_send(w.at[:, :, :, :, c, :, cols], f_send.at[i])


def body(tokens, out_grad, next_tokens, overflow, master, first_moment, second_moment):
    toks, din = tokens.shape
    rows, kv = master.shape
    ca, cb = 3 * kv // 8, 6 * kv // 8
    cx, cy, cz = ca, cb - ca, kv - cb
    width = NX * NL * NC * rows
    vmem, anym = pl.BlockSpec(memory_space=pltpu.VMEM), pl.BlockSpec(memory_space=pl.ANY)
    dma = pltpu.SemaphoreType.DMA
    shapes = (
        jax.ShapeDtypeStruct((rows, kv), F32),
        jax.ShapeDtypeStruct((rows, kv), F32),
        jax.ShapeDtypeStruct((rows, kv), F32),
        jax.ShapeDtypeStruct((NH, NY, NX, rows, kv), BF16),
        jax.ShapeDtypeStruct((toks, kv), BF16),
    )
    scratch = [
        pltpu.VMEM((NH * NY, toks, width), BF16),
        pltpu.VMEM((toks, kv), BF16),
        pltpu.VMEM((toks, din), BF16),
        pltpu.VMEM((NH, NY, NX, NL, rows, kv), F32),
        pltpu.VMEM((NH, NY, NX, NL, rows, kv), BF16),
        pltpu.VMEM((NH, NY, NX, NL, rows, kv), BF16),
        pltpu.VMEM((NH, NY, NX, NL, rows, kv), BF16),
        pltpu.VMEM((NX - 1, NH, NY, NL, rows, cx), BF16),
        pltpu.VMEM((NY - 1, NH, NX, NL, rows, cy), BF16),
        pltpu.VMEM((NZ - 1, NY, NX, rows, cz), BF16),
        pltpu.VMEM((NH, NY, NL, rows, cx), BF16),
        pltpu.VMEM((NH, NX, NL, rows, cy), BF16),
        pltpu.VMEM((NY, NX, rows, cz), BF16),
        pltpu.VMEM((NY - 1, NH, NL, rows, cx), BF16),
        pltpu.VMEM((NX - 1, NH, NL, rows, cy), BF16),
        pltpu.VMEM((NX - 1, NY, rows, cz), BF16),
        pltpu.VMEM((NH, NL, rows, cx + cy), BF16),
        pltpu.VMEM((NY, rows, cz), BF16),
        pltpu.VMEM((NZ - 1, rows, cx + cy), BF16),
        pltpu.VMEM((NY - 1, rows, cz), BF16),
        pltpu.VMEM((4, 8, 128), F32),
        pltpu.VMEM((1 + NX - 1 + NY - 1 + NZ - 1, 8, 128), F32),
        pltpu.VMEM((NH, NY, NX, NL, NC, rows, kv), BF16),
        pltpu.VMEM((toks, kv), F32),
    ]
    sems = (
        [2, NH * NY, 1, 1, NH * NY, 4, NX + NY + NZ - 2]
        + [3, NX - 1, NY - 1, NZ - 1]
        + [3, NY - 1, NX - 1, NX - 1]
        + [2, NZ - 1, NY - 1]
        + [2, NZ - 1, NY - 1]
        + [3, NY - 1, NX - 1, NX - 1]
        + [3, NX - 1, NY - 1, NZ - 1]
        + [3, NX, NY, NZ]
    )
    new_master, new_first, new_second, sec, proj = pl.pallas_call(
        kernel,
        out_shape=shapes,
        in_specs=[pl.BlockSpec(memory_space=pltpu.SMEM), anym, anym, anym, vmem, vmem, vmem],
        out_specs=(vmem, vmem, vmem, anym, vmem),
        scratch_shapes=scratch + [dma((n,)) for n in sems],
        compiler_params=pltpu.CompilerParams(
            collective_id=0, has_side_effects=True, vmem_limit_bytes=58 * 2**20
        ),
        cost_estimate=pl.CostEstimate(flops=4 * toks * din * kv, bytes_accessed=12 * 2**20, transcendentals=rows * kv),
    )(overflow, tokens, out_grad, next_tokens, master, first_moment, second_moment)
    return (new_master, new_first, new_second, sec.reshape(NH * NY * NX, rows, kv), proj)


def solution(mesh):
    return jax.shard_map(
        body,
        mesh=mesh,
        in_specs=(
            P(("node", "local"), None),
            P(("node", "local"), None),
            P(("node", "local"), None),
            P(("node", "local")),
            P(("node", "local"), None),
            P(("node", "local"), None),
            P(("node", "local"), None),
        ),
        out_specs=(
            P(("node", "local"), None),
            P(("node", "local"), None),
            P(("node", "local"), None),
            P(None, "local", None),
            P(("node", "local"), None),
        ),
        check_vma=False,
    )
```

time: 1520 us -> 108 us (0.07)
  the two profiles are of different devices: /device:TPU:1 before, /device:TPU:17 now
where the time goes in v1:
time: 108 us
  Pallas kernels  97.8 us (91%)
  local copies, waits for them, and re-layouts  8.98 us (8%)
  between operations  1.29 us (1%)
    pallas_call x1, Pallas kernels, body(): pl.pallas_call(kernel, out_shape=shapes, in_specs=[pl.BlockSpec(memory_sp...  97.8 us
    unnamed x5, local copies, waits for them, and re-layouts  8.98 us

profile of v1, /device:TPU:17, one launch (start us, length us, event | category | flops | bytes accessed | tf_op | source)
XLA Modules:
  0.0 108.1 jit_solution(9234357496435257766)
XLA Ops:
  1.3 97.8 %shard_map.110 = (f32[16,1024]{1,0:T(8,128)}, f32[16,1024]{1,0:T(8,128)}, f32[16,1024]{1,0:T(8,128)}, bf16[2,4,4,16,1024]{4,3,2,1,0:T(8,128)(2,1)}, bf16[512,1024]{1,0:T(8,128)(2,1)}) custom-call(s32[1]{0:T(128)S(6)} %copy.17.ov, bf16[512,4096]{1,0:T(8,128)(2,1)} %tok_hbm.1, bf16[512,1024]{1,0:T(8,128)(2,1)} %og_hbm.1, bf16[512,4096]{1,0:T(8,128)(2,1)} %nxt_hbm.1, ...), custom_call_target="tpu_custom_call" | custom-call | flops 8589934592 | bytes 12582912 | tf_op jit(solution)/shard_map/pallas_call | solution.py:401
  99.1 1.5 %copy.18 = f32[16,1024]{1,0:T(8,128)} copy(f32[16,1024]{1,0:T(8,128)} %get-tuple-element.20) | data formatting | bytes 131072
  100.6 1.5 %copy.19 = f32[16,1024]{1,0:T(8,128)} copy(f32[16,1024]{1,0:T(8,128)} %get-tuple-element.21) | data formatting | bytes 131072
  102.0 1.5 %copy.20 = f32[16,1024]{1,0:T(8,128)} copy(f32[16,1024]{1,0:T(8,128)} %get-tuple-element.22) | data formatting | bytes 131072
  103.5 2.3 %copy.21 = bf16[32,16,1024]{2,1,0:T(8,128)(2,1)} copy(bf16[32,16,1024]{2,1,0:T(8,128)(2,1)} %bitcast.1) | data formatting | bytes 2097152
  105.8 2.3 %copy.22 = bf16[512,1024]{1,0:T(8,128)(2,1)} copy(bf16[512,1024]{1,0:T(8,128)(2,1)} %get-tuple-element.24) | data formatting | bytes 2097152

commit v2 on v1

--- a/solution.py
+++ b/solution.py
@@ -18,10 +18,10 @@
     ov, tok_hbm, og_hbm, nxt_hbm, master, first, second,
     o_master, o_first, o_second, o_sec, o_proj,
     tok, og, nxt, own, sib_out, sib_in, s1,
-    r1x, r1y, r1z, s2x, s2y, s2z, r2x, r2y, r2z, s3a, s3z, r3a, r3z,
+    m1x, m1y, f1x, f1y, f1z, r1x, r1y, r1z, s2x, s2y, s2z, r2x, r2y, r2z, s3a, s3z, r3a, r3z,
     cnt, cnt_in, w, acc,
-    in_sem, tok_sem, out_sem, sib_send, sib_recv, cnt_send, cnt_recv,
-    p1_send, p1x_recv, p1y_recv, p1z_recv,
+    in_sem, tok_sem, nxt_sem, out_sem, sib_send, sib_recv, cnt_send, cnt_recv,
+    p1_send, m1x_recv, m1y_recv, p1x_recv, p1y_recv, p1z_recv,
     p2_send, p2x_recv, p2y_recv, p2z_recv, p3_send, p3a_recv, p3z_recv,
     a3_send, a3a_recv, a3z_recv, a2_send, a2x_recv, a2y_recv, a2z_recv,
     a1_send, a1x_recv, a1y_recv, a1z_recv, f_send, fx_recv, fy_recv, fz_recv,
@@ -48,6 +48,14 @@
     def ls(f):
         return lax.rem(l + f, NL)
 
+    def zdev(k):
+        zz = lax.rem(h * NL + l + k + NZ, NZ)
+        return dev(hh=lax.div(zz, NL), ll=lax.rem(zz, NL))
+
+    def zat(k):
+        zz = lax.rem(h * NL + l + k + NZ, NZ)
+        return lax.div(zz, NL), lax.rem(zz, NL)
+
     xd, yd = range(1, NX), range(1, NY)
     zd = [(e, f) for e in range(NH) for f in range(NL)][1:]
     sib = dev(cc=1 - c)
@@ -64,13 +72,17 @@
         remote(ref, ref, sem, sem, sib).wait_send()
 
     og_copy = pltpu.make_async_copy(og_hbm, og, in_sem.at[0])
-    nxt_copy = pltpu.make_async_copy(nxt_hbm, nxt, in_sem.at[1])
+
+    def nxt_copy(i):
+        cols = pl.ds(pl.multiple_of(i * NL * NC * rows, NL * NC * rows), NL * NC * rows)
+        return pltpu.make_async_copy(nxt_hbm.at[:, cols], nxt.at[i], nxt_sem.at[i])
+
     og_copy.start()
     width = NX * NL * NC * rows
     steps = NH * NY
 
     def place(it):
-        e, d = lax.rem(it, NH), lax.rem(lax.div(it, NH) + 1, NY)
+        e, d = lax.rem(it, NH), lax.rem(2 + NY - lax.div(it, NH), NY)
         return e, d, hs(e), ys(d)
 
     def tok_copy(it):
@@ -82,7 +94,10 @@
     def _(it):
         tok_copy(it).start()
 
-    nxt_copy.start()
+    @pl.loop(0, NH * NY * NX)
+    def _(i):
+        nxt_copy(i).start()
+
     peers = [sib]
     peers += [dev(xx=xs(d)) for d in xd] + [dev(yy=ys(d)) for d in yd]
     peers += [dev(hh=hs(e), ll=ls(f)) for e, f in zd]
@@ -100,33 +115,39 @@
         e, d, hh, yy = place(it)
         wait_recv(sib_in.at[hh, yy], sib_recv.at[it])
         s1[hh, yy] = (own[hh, yy] + sib_in[hh, yy].astype(F32)).astype(BF16)
-        for k in xd:
-            remote(
-                s1.at[hh, yy, xs(k), :, :, colx], r1x.at[k - 1, hh, yy],
-                p1_send.at[0], p1x_recv.at[k - 1], dev(xx=xs(k)),
-            ).start()
-
-        @pl.when(d > 0)
+        go, back = 1 + 2 * hh, NX - 1 - 2 * hh
+        remote(
+            s1.at[hh, yy, xs(2), :, :, colx], m1x.at[hh, yy], p1_send.at[0], m1x_recv.at[hh, yy], dev(xx=xs(go))
+        ).start()
+        remote(
+            s1.at[hh, yy, xs(back), :, :, colx], r1x.at[0, hh, yy], p1_send.at[1], p1x_recv.at[0], dev(xx=xs(back))
+        ).start()
+
+        @pl.when(d == 2)
         def _():
             remote(
-                s1.at[hh, yy, :, :, :, coly], r1y.at[d - 1, hh],
-                p1_send.at[1], p1y_recv.at[d - 1], dev(yy=yy),
+                s1.at[hh, yy, :, :, :, coly], m1y.at[hh], p1_send.at[3], m1y_recv.at[hh], dev(yy=ys(go))
             ).start()
 
-        def send_z(f):
-            ll = ls(f)
-            slot = e * NL + f - 1
+        @pl.when(d == back)
+        def _():
             remote(
-                s1.at[hh, yy, :, ll, :, colz], r1z.at[slot, yy],
-                p1_send.at[2], p1z_recv.at[slot], dev(hh=hh, ll=ll),
+                s1.at[hh, yy, :, :, :, coly], r1y.at[0, hh], p1_send.at[4], p1y_recv.at[0], dev(yy=ys(back))
             ).start()
 
-        for f in range(1, NL):
-            send_z(f)
-
-        @pl.when(e > 0)
-        def _():
-            send_z(0)
+        @pl.loop(0, NL)
+        def _(ll):
+            k = lax.rem(hh * NL + ll + NZ - h * NL - l, NZ)
+            up = k < 4
+            odd = lax.rem(k, 2) == 1
+            slot = jnp.where(odd, jnp.where((k == 1) | (k == 7), 0, 2) + jnp.where(up, 0, 1), 4)
+            hop = jnp.where(odd, jnp.where(up, 1, NZ - 1), jnp.where(yy < NY // 2, 2, NZ - 2))
+
+            @pl.when(odd | (k == 4))
+            def _():
+                remote(
+                    s1.at[hh, yy, :, ll, :, colz], r1z.at[slot, yy], p1_send.at[6], p1z_recv.at[slot], zdev(hop)
+                ).start()
 
     @pl.loop(0, steps)
     def _(it):
@@ -150,42 +171,72 @@
     for k in xd:
         remote(cnt.at[1], cnt_in.at[k], cnt_send.at[1], cnt_recv.at[k], dev(xx=xs(k))).start()
 
-    for k in xd:
-        wait_recv(r1x.at[k - 1], p1x_recv.at[k - 1])
+    @pl.loop(0, steps)
+    def _(it):
+        _, _, hh, yy = place(it)
+        go = 1 + 2 * hh
+        wait_recv(m1x.at[hh, yy], m1x_recv.at[hh, yy])
+        f1x[hh, yy] = (s1[hh, yy, xs(go), :, :, colx].astype(F32) + m1x[hh, yy].astype(F32)).astype(BF16)
+        remote(f1x.at[hh, yy], r1x.at[1, hh, yy], p1_send.at[2], p1x_recv.at[1], dev(xx=xs(go))).start()
+
+    @pl.loop(0, NH)
+    def _(hh):
+        go = 1 + 2 * hh
+        wait_recv(m1y.at[hh], m1y_recv.at[hh])
+
+        @pl.loop(0, NX)
+        def _(xx):
+            f1y[hh, xx] = (s1[hh, ys(go), xx, :, :, coly].astype(F32) + m1y[hh, xx].astype(F32)).astype(BF16)
+
+        remote(f1y.at[hh], r1y.at[1, hh], p1_send.at[5], p1y_recv.at[1], dev(yy=ys(go))).start()
+
+    for slot in (2, 3, 4):
+        wait_recv(r1z.at[slot], p1z_recv.at[slot])
+    for i, k in ((0, 2), (1, NZ - 2)):
+        hh, ll = zat(k)
+        for yy in range(NY):
+            total = s1[hh, yy, :, ll, :, colz].astype(F32) + r1z[2 + i, yy].astype(F32)
+            if (yy < NY // 2) == (i == 0):
+                total += r1z[4, yy].astype(F32)
+            f1z[i, yy] = total.astype(BF16)
+        remote(f1z.at[i], r1z.at[5 + i], p1_send.at[7], p1z_recv.at[5 + i], zdev(k)).start()
+
+    for k in range(2):
+        wait_recv(r1x.at[k], p1x_recv.at[k])
 
     @pl.loop(0, NH * NY)
     def _(i):
         hh, yy = lax.div(i, NY), lax.rem(i, NY)
         total = s1[hh, yy, x, :, :, colx].astype(F32)
-        for k in xd:
-            total += r1x[k - 1, hh, yy].astype(F32)
+        for k in range(2):
+            total += r1x[k, hh, yy].astype(F32)
         s2x[hh, yy] = total.astype(BF16)
 
     for k in yd:
         remote(s2x.at[:, ys(k)], r2x.at[k - 1], p2_send.at[0], p2x_recv.at[k - 1], dev(yy=ys(k))).start()
 
-    for k in yd:
-        wait_recv(r1y.at[k - 1], p1y_recv.at[k - 1])
+    for k in range(2):
+        wait_recv(r1y.at[k], p1y_recv.at[k])
 
     @pl.loop(0, NH * NX)
     def _(i):
         hh, xx = lax.div(i, NX), lax.rem(i, NX)
         total = s1[hh, y, xx, :, :, coly].astype(F32)
-        for k in yd:
-            total += r1y[k - 1, hh, xx].astype(F32)
+        for k in range(2):
+            total += r1y[k, hh, xx].astype(F32)
         s2y[hh, xx] = total.astype(BF16)
 
     for k in xd:
         remote(s2y.at[:, xs(k)], r2y.at[k - 1], p2_send.at[1], p2y_recv.at[k - 1], dev(xx=xs(k))).start()
 
-    for k in range(1, NZ):
-        wait_recv(r1z.at[k - 1], p1z_recv.at[k - 1])
+    for k in (0, 1, 5, 6):
+        wait_recv(r1z.at[k], p1z_recv.at[k])
 
     @pl.loop(0, NY)
     def _(yy):
         total = s1[h, yy, :, l, :, colz].astype(F32)
-        for k in range(1, NZ):
-            total += r1z[k - 1, yy].astype(F32)
+        for k in (0, 1, 5, 6):
+            total += r1z[k, yy].astype(F32)
         s2z[yy] = total.astype(BF16)
 
     for k in xd:
@@ -280,53 +331,119 @@
     for k in xd:
         gather(w.at[h, :, x, l, c, :, colz], a2_send.at[2], a2z_recv.at[k - 1], dev(xx=xs(k)))
 
+    def xpart(k, hh):
+        return w.at[hh, :, xs(k), :, c, :, colx]
+
+    def ypart(k, hh):
+        return w.at[hh, ys(k), :, :, c, :, coly]
+
+    def zpart(k):
+        hh, ll = zat(k)
+        return w.at[hh, :, :, ll, c, :, colz]
+
+    def zhalf(k, i):
+        hh, ll = zat(k)
+        return w.at[hh, pl.ds(i * (NY // 2), NY // 2), :, ll, c, :, colz]
+
     for k in yd:
         wait_recv(r2x.at[k - 1], a2x_recv.at[k - 1])
-    for k in xd:
-        gather(w.at[:, :, x, :, c, :, colx], a1_send.at[0], a1x_recv.at[k - 1], dev(xx=xs(k)))
+    for i in range(2):
+        gather(xpart(0, i), a1_send.at[0], a1x_recv.at[i, 0], dev(xx=xs(1 + 2 * i)))
+    for i in range(2):
+        gather(xpart(0, i), a1_send.at[0], a1x_recv.at[i, 1], dev(xx=xs(3 - 2 * i)))
     for k in xd:
         wait_recv(r2y.at[k - 1], a2y_recv.at[k - 1])
-    for k in yd:
-        gather(w.at[:, y, :, :, c, :, coly], a1_send.at[1], a1y_recv.at[k - 1], dev(yy=ys(k)))
+    for i in range(2):
+        gather(ypart(0, i), a1_send.at[2], a1y_recv.at[i, 0], dev(yy=ys(1 + 2 * i)))
+    for i in range(2):
+        gather(ypart(0, i), a1_send.at[2], a1y_recv.at[i, 1], dev(yy=ys(3 - 2 * i)))
     for k in xd:
         wait_recv(r2z.at[k - 1], a2z_recv.at[k - 1])
-    for e, f in zd:
-        gather(w.at[h, :, :, l, c, :, colz], a1_send.at[2], a1z_recv.at[e * NL + f - 1], dev(hh=hs(e), ll=ls(f)))
-
-    gather(w.at[:, :, x, :, c, :, colx], f_send.at[0], fx_recv.at[0], sib)
-    gather(w.at[:, y, :, :, c, :, coly], f_send.at[1], fy_recv.at[0], sib)
-    gather(w.at[h, :, :, l, c, :, colz], f_send.at[2], fz_recv.at[0], sib)
-    for k in xd:
-        wait_recv(r1x.at[k - 1], a1x_recv.at[k - 1])
-        gather(w.at[:, :, xs(NX - k), :, c, :, colx], f_send.at[0], fx_recv.at[k], sib)
-    for k in yd:
-        wait_recv(r1y.at[k - 1], a1y_recv.at[k - 1])
-        gather(w.at[:, ys(NY - k), :, :, c, :, coly], f_send.at[1], fy_recv.at[k], sib)
-    for e, f in zd:
-        slot = e * NL + f - 1
-        wait_recv(r1z.at[slot], a1z_recv.at[slot])
-        gather(w.at[hs(NH - e), :, :, ls(NL - f), c, :, colz], f_send.at[2], fz_recv.at[slot + 1], sib)
-
+    for slot, k in enumerate((2, -2, 1, -1)):
+        gather(zpart(0), a1_send.at[4], a1z_recv.at[slot], zdev(k))
+    for i in range(2):
+        gather(xpart(0, i), f_send.at[0], fx_recv.at[0], sib)
+        gather(ypart(0, i), f_send.at[1], fy_recv.at[0], sib)
+    gather(zpart(0), f_send.at[2], fz_recv.at[0], sib)
+
+    for i in range(2):
+        wait_recv(m1x.at[0], a1x_recv.at[i, 0])
+        gather(xpart(3 - 2 * i, i), a1_send.at[1], a1x_recv.at[i, 2], dev(xx=xs(1 + 2 * i)))
+        wait_recv(m1y.at[0], a1y_recv.at[i, 0])
+        gather(ypart(3 - 2 * i, i), a1_send.at[3], a1y_recv.at[i, 2], dev(yy=ys(1 + 2 * i)))
+    for i, k in enumerate((-2, 2)):
+        wait_recv(r1z.at[0], a1z_recv.at[i])
+        gather(zhalf(k, i), a1_send.at[5], a1z_recv.at[4 + i], zdev(-k))
+        gather(zpart(k), a1_send.at[5], a1z_recv.at[6 + i], zdev(-k // 2))
+    for i in range(2):
+        gather(xpart(3 - 2 * i, i), f_send.at[0], fx_recv.at[3 - 2 * i], sib)
+        gather(ypart(3 - 2 * i, i), f_send.at[1], fy_recv.at[3 - 2 * i], sib)
+    for k in (-2, 2):
+        gather(zpart(k), f_send.at[2], fz_recv.at[0], sib)
+
+    def project_x(k):
+        for hh in range(NH):
+            lhs = jnp.concatenate([nxt[(hh * NY + yy) * NX + xs(k)] for yy in range(NY)], axis=1)
+            rhs = w[hh, :, xs(k), :, :, :, colx].reshape(NY * NL * NC * rows, ca)
+            acc[:, colx] += jnp.dot(lhs, rhs, preferred_element_type=F32)
+
+    def project_y(k):
+        for hh in range(NH):
+            lhs = jnp.concatenate([nxt[(hh * NY + ys(k)) * NX + xx] for xx in range(NX)], axis=1)
+            rhs = w[hh, ys(k), :, :, :, :, coly].reshape(NX * NL * NC * rows, cb - ca)
+            acc[:, coly] += jnp.dot(lhs, rhs, preferred_element_type=F32)
+
+    acc[...] = jnp.zeros_like(acc)
+
+    @pl.loop(0, NH * NY * NX)
+    def _(i):
+        nxt_copy(i).wait()
+
+    wait_recv(r1x.at[0], fx_recv.at[0])
+    project_x(0)
+    for i in range(2):
+        wait_recv(m1x.at[0], a1x_recv.at[i, 1])
+        gather(xpart(1 + 2 * i, i), f_send.at[0], fx_recv.at[1 + 2 * i], sib)
+        wait_recv(m1y.at[0], a1y_recv.at[i, 1])
+        gather(ypart(1 + 2 * i, i), f_send.at[1], fy_recv.at[1 + 2 * i], sib)
+    wait_recv(r1y.at[0], fy_recv.at[0])
+    project_y(0)
+    for i, k in enumerate((-1, 1)):
+        wait_recv(r1z.at[0], a1z_recv.at[2 + i])
+        gather(zpart(k), f_send.at[2], fz_recv.at[0], sib)
+    for k in (1, 3):
+        wait_recv(r1x.at[0], fx_recv.at[k])
+        project_x(k)
+        wait_recv(r1y.at[0], fy_recv.at[k])
+        project_y(k)
+    for i in range(2):
+        wait_recv(m1x.at[0], a1x_recv.at[i, 2])
+        gather(xpart(2, i), f_send.at[0], fx_recv.at[2], sib)
+        wait_recv(m1y.at[0], a1y_recv.at[i, 2])
+        gather(ypart(2, i), f_send.at[1], fy_recv.at[2], sib)
+    for i, k in enumerate((-3, 3)):
+        wait_recv(r1z.at[0], a1z_recv.at[6 + i])
+        gather(zpart(k), f_send.at[2], fz_recv.at[0], sib)
+    for i in range(2):
+        wait_recv(r1z.at[0, pl.ds(0, NY // 2)], a1z_recv.at[4 + i])
+        gather(zhalf(4, i), f_send.at[2], fz_recv.at[0], sib)
     sec_copy = pltpu.make_async_copy(w.at[:, :, :, l, c], o_sec, out_sem.at[0])
     sec_copy.start()
-
-    nxt_copy.wait()
-    for k in range(NX):
-        wait_recv(r1x.at[0], fx_recv.at[k])
-    for k in range(NY):
-        wait_recv(r1y.at[0], fy_recv.at[k])
-    for k in range(NZ):
-        wait_recv(r1z.at[0], fz_recv.at[k])
-
-    acc[...] = jnp.zeros_like(acc)
+    wait_recv(r1x.at[0], fx_recv.at[2])
+    project_x(2)
+    o_proj[:, colx] = acc[:, colx].astype(BF16)
+    wait_recv(r1y.at[0], fy_recv.at[2])
+    project_y(2)
+    o_proj[:, coly] = acc[:, coly].astype(BF16)
+    wait_recv(w.at[:, :, :, :, 1 - c, :, colz], fz_recv.at[0])
 
     @pl.loop(0, steps)
     def _(i):
         hh, yy = lax.div(i, NY), lax.rem(i, NY)
-        cols = pl.ds(pl.multiple_of(i * width, width), width)
-        acc[...] += jnp.dot(nxt[:, cols], w[hh, yy].reshape(width, kv), preferred_element_type=F32)
-
-    o_proj[...] = acc[...].astype(BF16)
+        lhs = jnp.concatenate([nxt[i * NX + xx] for xx in range(NX)], axis=1)
+        acc[:, colz] += jnp.dot(lhs, w[hh, yy, :, :, :, :, colz].reshape(width, kv - cb), preferred_element_type=F32)
+
+    o_proj[:, colz] = acc[:, colz].astype(BF16)
     sec_copy.wait()
 
     wait_send(sib_out, sib_send.at[0])
@@ -334,8 +451,9 @@
     wait_send(cnt_in.at[pl.ds(0, NX - 1)], cnt_send.at[1])
     wait_send(cnt_in.at[pl.ds(0, NY - 1)], cnt_send.at[2])
     wait_send(cnt_in.at[pl.ds(0, NZ - 1)], cnt_send.at[3])
-    for i, ref in enumerate((r1x, r1y, r1z)):
+    for i, ref in enumerate((m1x, r1x.at[0], r1x.at[1], m1y, r1y.at[0], r1y.at[1], r1z.at[pl.ds(0, 5)], f1z)):
         wait_send(ref, p1_send.at[i])
+    for i, ref in enumerate((r1x, r1x.at[0], r1y, r1y.at[0], r1z.at[pl.ds(0, 4)], r1z.at[pl.ds(0, 3)])):
         wait_send(ref, a1_send.at[i])
     for i, ref in enumerate((r2x, r2y, r2z)):
         wait_send(ref, p2_send.at[i])
@@ -345,6 +463,15 @@
         wait_send(ref, a3_send.at[i])
     for i, cols in enumerate((colx, coly, colz)):
         wait_send(w.at[:, :, :, :, c, :, cols], f_send.at[i])
+
+
+def copy_out(*refs):
+    sem = refs[-1]
+    copies = [pltpu.make_async_copy(refs[i], refs[5 + i], sem.at[i]) for i in range(5)]
+    for copy in copies:
+        copy.start()
+    for copy in copies:
+        copy.wait()
 
 
 def body(tokens, out_grad, next_tokens, overflow, master, first_moment, second_moment):
@@ -365,14 +492,19 @@
     scratch = [
         pltpu.VMEM((NH * NY, toks, width), BF16),
         pltpu.VMEM((toks, kv), BF16),
-        pltpu.VMEM((toks, din), BF16),
+        pltpu.VMEM((NH * NY * NX, toks, NL * NC * rows), BF16),
         pltpu.VMEM((NH, NY, NX, NL, rows, kv), F32),
         pltpu.VMEM((NH, NY, NX, NL, rows, kv), BF16),
         pltpu.VMEM((NH, NY, NX, NL, rows, kv), BF16),
         pltpu.VMEM((NH, NY, NX, NL, rows, kv), BF16),
-        pltpu.VMEM((NX - 1, NH, NY, NL, rows, cx), BF16),
-        pltpu.VMEM((NY - 1, NH, NX, NL, rows, cy), BF16),
-        pltpu.VMEM((NZ - 1, NY, NX, rows, cz), BF16),
+        pltpu.VMEM((NH, NY, NL, rows, cx), BF16),
+        pltpu.VMEM((NH, NX, NL, rows, cy), BF16),
+        pltpu.VMEM((NH, NY, NL, rows, cx), BF16),
+        pltpu.VMEM((NH, NX, NL, rows, cy), BF16),
+        pltpu.VMEM((2, NY, NX, rows, cz), BF16),
+        pltpu.VMEM((2, NH, NY, NL, rows, cx), BF16),
+        pltpu.VMEM((2, NH, NX, NL, rows, cy), BF16),
+        pltpu.VMEM((7, NY, NX, rows, cz), BF16),
         pltpu.VMEM((NH, NY, NL, rows, cx), BF16),
         pltpu.VMEM((NH, NX, NL, rows, cy), BF16),
         pltpu.VMEM((NY, NX, rows, cz), BF16),
@@ -389,26 +521,33 @@
         pltpu.VMEM((toks, kv), F32),
     ]
     sems = (
-        [2, NH * NY, 1, 1, NH * NY, 4, NX + NY + NZ - 2]
-        + [3, NX - 1, NY - 1, NZ - 1]
-        + [3, NY - 1, NX - 1, NX - 1]
-        + [2, NZ - 1, NY - 1]
-        + [2, NZ - 1, NY - 1]
-        + [3, NY - 1, NX - 1, NX - 1]
-        + [3, NX - 1, NY - 1, NZ - 1]
-        + [3, NX, NY, NZ]
+        [(1,), (NH * NY,), (NH * NY * NX,), (1,), (1,), (NH * NY,), (4,), (NX + NY + NZ - 2,)]
+        + [(8,), (NH, NY), (NH,), (2,), (2,), (7,)]
+        + [(3,), (NY - 1,), (NX - 1,), (NX - 1,)]
+        + [(2,), (NZ - 1,), (NY - 1,)]
+        + [(2,), (NZ - 1,), (NY - 1,)]
+        + [(3,), (NY - 1,), (NX - 1,), (NX - 1,)]
+        + [(6,), (2, 3), (2, 3), (8,)]
+        + [(3,), (NX,), (NY,), (1,)]
     )
-    new_master, new_first, new_second, sec, proj = pl.pallas_call(
+    results = pl.pallas_call(
         kernel,
         out_shape=shapes,
         in_specs=[pl.BlockSpec(memory_space=pltpu.SMEM), anym, anym, anym, vmem, vmem, vmem],
         out_specs=(vmem, vmem, vmem, anym, vmem),
-        scratch_shapes=scratch + [dma((n,)) for n in sems],
+        scratch_shapes=scratch + [dma(n) for n in sems],
         compiler_params=pltpu.CompilerParams(
             collective_id=0, has_side_effects=True, vmem_limit_bytes=58 * 2**20
         ),
         cost_estimate=pl.CostEstimate(flops=4 * toks * din * kv, bytes_accessed=12 * 2**20, transcendentals=rows * kv),
     )(overflow, tokens, out_grad, next_tokens, master, first_moment, second_moment)
+    new_master, new_first, new_second, sec, proj = pl.pallas_call(
+        copy_out,
+        out_shape=shapes,
+        in_specs=[anym] * 5,
+        out_specs=[anym] * 5,
+        scratch_shapes=[dma((5,))],
+    )(*results)
     return (new_master, new_first, new_second, sec.reshape(NH * NY * NX, rows, kv), proj)
 
 

time: 108 us -> 154 us (1.43)
  the two profiles are of different devices: /device:TPU:17 before, /device:TPU:1 now
where the time goes in v2:
time: 154 us; the launch traced here: 153 us
  Pallas kernels  152 us (99%)
    pallas_call x1, Pallas kernels, body(): pl.pallas_call(kernel, out_shape=shapes, in_specs=[pl.BlockSpec(memory_sp...  81.4 us
    pallas_call x1, Pallas kernels, body(): pl.pallas_call(copy_out, out_shape=shapes, in_specs=[anym] * 5, out_specs...  70.6 us

profile of v2, /device:TPU:1, one launch (start us, length us, event | category | flops | bytes accessed | tf_op | source)
XLA Modules:
  0.0 153.4 jit_solution(6352179319576551928)
XLA Ops:
  1.3 81.4 %shard_map.110 = (f32[16,1024]{1,0:T(8,128)}, f32[16,1024]{1,0:T(8,128)}, f32[16,1024]{1,0:T(8,128)}, bf16[2,4,4,16,1024]{4,3,2,1,0:T(8,128)(2,1)}, bf16[512,1024]{1,0:T(8,128)(2,1)}) custom-call(s32[1]{0:T(128)S(6)} %copy.12.ov, bf16[512,4096]{1,0:T(8,128)(2,1)} %tok_hbm.1, bf16[512,1024]{1,0:T(8,128)(2,1)} %og_hbm.1, bf16[512,4096]{1,0:T(8,128)(2,1)} %nxt_hbm.1, ...), custom_call_target="tpu_custom_call" | custom-call | flops 8589934592 | bytes 12582912 | tf_op jit(solution)/shard_map/pallas_call | solution.py:533
  82.7 70.6 %shard_map.111 = (f32[16,1024]{1,0:T(8,128)}, f32[16,1024]{1,0:T(8,128)}, f32[16,1024]{1,0:T(8,128)}, bf16[2,4,4,16,1024]{4,3,2,1,0:T(8,128)(2,1)}, bf16[512,1024]{1,0:T(8,128)(2,1)}) custom-call(f32[16,1024]{1,0:T(8,128)} %get-tuple-element.15.refs_0_, f32[16,1024]{1,0:T(8,128)} %get-tuple-element.16.refs_1_, f32[16,1024]{1,0:T(8,128)} %get-tuple-element.17.refs_2_, ...), custom_call_target="tpu_custom_call" | custom-call | tf_op jit(solution)/shard_map/pallas_call | solution.py:544

commit v3 on v2

--- a/solution.py
+++ b/solution.py
@@ -11,6 +11,7 @@
 MESH = pl.DeviceIdType.MESH
 NH, NY, NX, NL, NC = 2, 4, 4, 4, 2
 NZ = NH * NL
+PARTS = (1, 1, 1, 2, 4)
 F32, BF16 = jnp.float32, jnp.bfloat16
 
 
@@ -71,6 +72,12 @@
     def wait_send(ref, sem):
         remote(ref, ref, sem, sem, sib).wait_send()
 
+    pending = []
+
+    def drain():
+        for ref, sem in pending:
+            wait_send(ref, sem)
+
     og_copy = pltpu.make_async_copy(og_hbm, og, in_sem.at[0])
 
     def nxt_copy(i):
@@ -171,6 +178,10 @@
     for k in xd:
         remote(cnt.at[1], cnt_in.at[k], cnt_send.at[1], cnt_recv.at[k], dev(xx=xs(k))).start()
 
+    pending += [(sib_out, sib_send.at[0]), (cnt.at[0], cnt_send.at[0]), (cnt_in.at[pl.ds(0, NX - 1)], cnt_send.at[1])]
+    pending += [(m1x, p1_send.at[0]), (r1x.at[0], p1_send.at[1]), (m1y, p1_send.at[3]), (r1y.at[0], p1_send.at[4])]
+    pending += [(r1z.at[pl.ds(0, 5)], p1_send.at[6])]
+
     @pl.loop(0, steps)
     def _(it):
         _, _, hh, yy = place(it)
@@ -201,6 +212,8 @@
             f1z[i, yy] = total.astype(BF16)
         remote(f1z.at[i], r1z.at[5 + i], p1_send.at[7], p1z_recv.at[5 + i], zdev(k)).start()
 
+    pending += [(f1x, p1_send.at[2]), (f1y, p1_send.at[5]), (f1z, p1_send.at[7])]
+
     for k in range(2):
         wait_recv(r1x.at[k], p1x_recv.at[k])
 
@@ -248,6 +261,9 @@
     for k in yd:
         remote(cnt.at[2], cnt_in.at[NX - 1 + k], cnt_send.at[2], cnt_recv.at[NX - 1 + k], dev(yy=ys(k))).start()
 
+    pending += [(r2x, p2_send.at[0]), (r2y, p2_send.at[1]), (r2z, p2_send.at[2])]
+    pending += [(cnt_in.at[pl.ds(0, NY - 1)], cnt_send.at[2])]
+
     for k in yd:
         wait_recv(r2x.at[k - 1], p2x_recv.at[k - 1])
     total = s2x[:, y].astype(F32)
@@ -298,6 +314,8 @@
     for k in range(1, NZ):
         count += cnt_in[base + k - 1]
     count = count[0:1, 0:1]
+
+    pending += [(r3a, p3_send.at[0]), (r3z, p3_send.at[1]), (cnt_in.at[pl.ds(0, NZ - 1)], cnt_send.at[3])]
 
     def adam(cols, summed):
         grad = summed / count
@@ -345,6 +363,9 @@
         hh, ll = zat(k)
         return w.at[hh, pl.ds(i * (NY // 2), NY // 2), :, ll, c, :, colz]
 
+    pending += [(r3a, a3_send.at[0]), (r3z, a3_send.at[1])]
+    pending += [(r2x, a2_send.at[0]), (r2y, a2_send.at[1]), (r2z, a2_send.at[2])]
+
     for k in yd:
         wait_recv(r2x.at[k - 1], a2x_recv.at[k - 1])
     for i in range(2):
@@ -380,6 +401,10 @@
         gather(ypart(3 - 2 * i, i), f_send.at[1], fy_recv.at[3 - 2 * i], sib)
     for k in (-2, 2):
         gather(zpart(k), f_send.at[2], fz_recv.at[0], sib)
+
+    pending += [(r1x, a1_send.at[0]), (r1x.at[0], a1_send.at[1]), (r1y, a1_send.at[2]), (r1y.at[0], a1_send.at[3])]
+    pending += [(r1z.at[pl.ds(0, 4)], a1_send.at[4]), (r1z.at[pl.ds(0, 3)], a1_send.at[5])]
+    pending += [(w.at[:, :, :, :, c, :, cols], f_send.at[i]) for i, cols in enumerate((colx, coly, colz))]
 
     def project_x(k):
         for hh in range(NH):
@@ -446,31 +471,24 @@
     o_proj[:, colz] = acc[:, colz].astype(BF16)
     sec_copy.wait()
 
-    wait_send(sib_out, sib_send.at[0])
-    wait_send(cnt.at[0], cnt_send.at[0])
-    wait_send(cnt_in.at[pl.ds(0, NX - 1)], cnt_send.at[1])
-    wait_send(cnt_in.at[pl.ds(0, NY - 1)], cnt_send.at[2])
-    wait_send(cnt_in.at[pl.ds(0, NZ - 1)], cnt_send.at[3])
-    for i, ref in enumerate((m1x, r1x.at[0], r1x.at[1], m1y, r1y.at[0], r1y.at[1], r1z.at[pl.ds(0, 5)], f1z)):
-        wait_send(ref, p1_send.at[i])
-    for i, ref in enumerate((r1x, r1x.at[0], r1y, r1y.at[0], r1z.at[pl.ds(0, 4)], r1z.at[pl.ds(0, 3)])):
-        wait_send(ref, a1_send.at[i])
-    for i, ref in enumerate((r2x, r2y, r2z)):
-        wait_send(ref, p2_send.at[i])
-        wait_send(ref, a2_send.at[i])
-    for i, ref in enumerate((r3a, r3z)):
-        wait_send(ref, p3_send.at[i])
-        wait_send(ref, a3_send.at[i])
-    for i, cols in enumerate((colx, coly, colz)):
-        wait_send(w.at[:, :, :, :, c, :, cols], f_send.at[i])
+    drain()
 
 
 def copy_out(*refs):
-    sem = refs[-1]
-    copies = [pltpu.make_async_copy(refs[i], refs[5 + i], sem.at[i]) for i in range(5)]
-    for copy in copies:
+    src, dst, held, sem_in, sem_out = refs[:5], refs[5:10], refs[10:15], refs[15], refs[16]
+    parts = []
+    for i in range(5):
+        rows = src[i].shape[0]
+        n = PARTS[i]
+        parts += [(i, pl.ds(j * rows // n, rows // n)) for j in range(n)]
+    reads = [pltpu.make_async_copy(src[i].at[r], held[i].at[r], sem_in.at[j]) for j, (i, r) in enumerate(parts)]
+    writes = [pltpu.make_async_copy(held[i].at[r], dst[i].at[r], sem_out.at[j]) for j, (i, r) in enumerate(parts)]
+    for copy in reads:
         copy.start()
-    for copy in copies:
+    for read, write in zip(reads, writes):
+        read.wait()
+        write.start()
+    for copy in writes:
         copy.wait()
 
 
@@ -546,7 +564,8 @@
         out_shape=shapes,
         in_specs=[anym] * 5,
         out_specs=[anym] * 5,
-        scratch_shapes=[dma((5,))],
+        scratch_shapes=[pltpu.VMEM(shape.shape, shape.dtype) for shape in shapes] + [dma((sum(PARTS),))] * 2,
+        compiler_params=pltpu.CompilerParams(vmem_limit_bytes=58 * 2**20),
     )(*results)
     return (new_master, new_first, new_second, sec.reshape(NH * NY * NX, rows, kv), proj)
 

time: 154 us -> 85.5 us (0.56)
  Pallas kernels: 152 us -> 84.1 us
    pallas_call x1, Pallas kernels: 70.6 us -> 2.62 us  [body(): pl.pallas_call(copy_out, out_shape=shapes, in_specs=[anym] * 5, out_specs...]
where the time goes in v3:
time: 85.5 us; the launch traced here: 85.4 us
  Pallas kernels  84.1 us (98%)
  between operations  1.29 us (2%)
    pallas_call x1, Pallas kernels, body(): pl.pallas_call(kernel, out_shape=shapes, in_specs=[pl.BlockSpec(memory_sp...  81.4 us
    pallas_call x1, Pallas kernels, body(): pl.pallas_call(copy_out, out_shape=shapes, in_specs=[anym] * 5, out_specs...  2.62 us

profile of v3, /device:TPU:1, one launch (start us, length us, event | category | flops | bytes accessed | tf_op | source)
XLA Modules:
  0.0 85.4 jit_solution(1763364557788210206)
XLA Ops:
  1.3 81.4 %shard_map.110 = (f32[16,1024]{1,0:T(8,128)}, f32[16,1024]{1,0:T(8,128)}, f32[16,1024]{1,0:T(8,128)}, bf16[2,4,4,16,1024]{4,3,2,1,0:T(8,128)(2,1)}, bf16[512,1024]{1,0:T(8,128)(2,1)}) custom-call(s32[1]{0:T(128)S(6)} %copy.12.ov, bf16[512,4096]{1,0:T(8,128)(2,1)} %tok_hbm.1, bf16[512,1024]{1,0:T(8,128)(2,1)} %og_hbm.1, bf16[512,4096]{1,0:T(8,128)(2,1)} %nxt_hbm.1, ...), custom_call_target="tpu_custom_call" | custom-call | flops 8589934592 | bytes 12582912 | tf_op jit(solution)/shard_map/pallas_call | solution.py:551
  82.7 2.6 %shard_map.111 = (f32[16,1024]{1,0:T(8,128)}, f32[16,1024]{1,0:T(8,128)}, f32[16,1024]{1,0:T(8,128)}, bf16[2,4,4,16,1024]{4,3,2,1,0:T(8,128)(2,1)}, bf16[512,1024]{1,0:T(8,128)(2,1)}) custom-call(f32[16,1024]{1,0:T(8,128)} %get-tuple-element.15.refs_0_, f32[16,1024]{1,0:T(8,128)} %get-tuple-element.16.refs_1_, f32[16,1024]{1,0:T(8,128)} %get-tuple-element.17.refs_2_, ...), custom_call_target="tpu_custom_call" | custom-call | tf_op jit(solution)/shard_map/pallas_call | solution.py:562

commit v4 on v3

--- a/solution.py
+++ b/solution.py
@@ -11,14 +11,15 @@
 MESH = pl.DeviceIdType.MESH
 NH, NY, NX, NL, NC = 2, 4, 4, 4, 2
 NZ = NH * NL
-PARTS = (1, 1, 1, 2, 4)
+LAG = 2
+PARTS = (1, 1, 1, 2, 2)
 F32, BF16 = jnp.float32, jnp.bfloat16
 
 
 def kernel(
-    ov, tok_hbm, og_hbm, nxt_hbm, master, first, second,
+    ov_hbm, tok_hbm, og_hbm, nxt_hbm, master_hbm, first_hbm, second_hbm,
     o_master, o_first, o_second, o_sec, o_proj,
-    tok, og, nxt, own, sib_out, sib_in, s1,
+    ov, master, first, second, tok, og, nxt, own, sib_out, sib_in, s1,
     m1x, m1y, f1x, f1y, f1z, r1x, r1y, r1z, s2x, s2y, s2z, r2x, r2y, r2z, s3a, s3z, r3a, r3z,
     cnt, cnt_in, w, acc,
     in_sem, tok_sem, nxt_sem, out_sem, sib_send, sib_recv, cnt_send, cnt_recv,
@@ -78,45 +79,67 @@
         for ref, sem in pending:
             wait_send(ref, sem)
 
-    og_copy = pltpu.make_async_copy(og_hbm, og, in_sem.at[0])
-
-    def nxt_copy(i):
-        cols = pl.ds(pl.multiple_of(i * NL * NC * rows, NL * NC * rows), NL * NC * rows)
-        return pltpu.make_async_copy(nxt_hbm.at[:, cols], nxt.at[i], nxt_sem.at[i])
-
-    og_copy.start()
-    width = NX * NL * NC * rows
-    steps = NH * NY
-
-    def place(it):
-        e, d = lax.rem(it, NH), lax.rem(2 + NY - lax.div(it, NH), NY)
-        return e, d, hs(e), ys(d)
-
-    def tok_copy(it):
-        _, _, hh, yy = place(it)
-        cols = pl.ds(pl.multiple_of((hh * NY + yy) * width, width), width)
-        return pltpu.make_async_copy(tok_hbm.at[:, cols], tok.at[it], tok_sem.at[it])
-
-    @pl.loop(0, steps)
-    def _(it):
-        tok_copy(it).start()
-
-    @pl.loop(0, NH * NY * NX)
-    def _(i):
-        nxt_copy(i).start()
-
     peers = [sib]
     peers += [dev(xx=xs(d)) for d in xd] + [dev(yy=ys(d)) for d in yd]
     peers += [dev(hh=hs(e), ll=ls(f)) for e, f in zd]
     barrier = pltpu.get_barrier_semaphore()
     for to in peers:
         pl.semaphore_signal(barrier, inc=1, device_id=to, device_id_type=MESH)
+
+    og_copy = pltpu.make_async_copy(og_hbm, og, in_sem.at[0])
+
+    def nxt_copy(i):
+        cols = pl.ds(pl.multiple_of(i * NL * NC * rows, NL * NC * rows), NL * NC * rows)
+        return pltpu.make_async_copy(nxt_hbm.at[:, cols], nxt.at[i], nxt_sem.at[i])
+
+    ov_copy = pltpu.make_async_copy(ov_hbm, ov, in_sem.at[1])
+    adam_copies = [
+        pltpu.make_async_copy(src, dst, in_sem.at[2 + i])
+        for i, (src, dst) in enumerate(((master_hbm, master), (first_hbm, first), (second_hbm, second)))
+    ]
+    og_copy.start()
+    ov_copy.start()
+    width = NX * NL * NC * rows
+    steps = NH * NY
+
+    def place(it):
+        e, d = lax.rem(it, NH), lax.rem(2 + NY - lax.div(it, NH), NY)
+        return e, d, hs(e), ys(d)
+
+    def tok_copy(it):
+        _, _, hh, yy = place(it)
+        cols = pl.ds(pl.multiple_of((hh * NY + yy) * width, width), width)
+        return pltpu.make_async_copy(tok_hbm.at[:, cols], tok.at[it], tok_sem.at[it])
+
+    @pl.loop(0, steps)
+    def _(it):
+        tok_copy(it).start()
+
+    for copy in adam_copies:
+        copy.start()
+    og_copy.wait()
+    ov_copy.wait()
     kept = (1 - ov[0]).astype(F32)
+    og[...] = og[...] * kept.astype(BF16)
     cnt[0] = jnp.full(cnt.shape[1:], kept, F32)
-    og_copy.wait()
-    og[...] = og[...] * kept.astype(BF16)
+
+    def partial_sum(it):
+        _, _, hh, yy = place(it)
+        tok_copy(it).wait()
+        part = lax.dot_general(tok[it], og[...], (((0,), (0,)), ((), ())), preferred_element_type=F32)
+        part = part.reshape(NX, NL, NC, rows, kv)
+        even, odd = part[:, :, 0], part[:, :, 1]
+        own[hh, yy] = jnp.where(c == 0, even, odd)
+        sib_out[hh, yy] = jnp.where(c == 0, odd, even).astype(BF16)
+
+    def send_partial(it):
+        _, _, hh, yy = place(it)
+        remote(sib_out.at[hh, yy], sib_in.at[hh, yy], sib_send.at[0], sib_recv.at[it], sib).start()
+
+    pl.loop(0, LAG)(partial_sum)
     pl.semaphore_wait(barrier, len(peers))
     remote(cnt.at[0], cnt_in.at[0], cnt_send.at[0], cnt_recv.at[0], sib).start()
+    pl.loop(0, LAG)(send_partial)
 
     def exchange_first(it):
         e, d, hh, yy = place(it)
@@ -142,7 +165,7 @@
                 s1.at[hh, yy, :, :, :, coly], r1y.at[0, hh], p1_send.at[4], p1y_recv.at[0], dev(yy=ys(back))
             ).start()
 
-        @pl.loop(0, NL)
+        @pl.loop(0, NL, unroll=True)
         def _(ll):
             k = lax.rem(hh * NL + ll + NZ - h * NL - l, NZ)
             up = k < 4
@@ -156,22 +179,13 @@
                     s1.at[hh, yy, :, ll, :, colz], r1z.at[slot, yy], p1_send.at[6], p1z_recv.at[slot], zdev(hop)
                 ).start()
 
-    @pl.loop(0, steps)
+    @pl.loop(LAG, steps)
     def _(it):
-        _, _, hh, yy = place(it)
-        tok_copy(it).wait()
-        part = lax.dot_general(tok[it], og[...], (((0,), (0,)), ((), ())), preferred_element_type=F32)
-        part = part.reshape(NX, NL, NC, rows, kv)
-        even, odd = part[:, :, 0], part[:, :, 1]
-        own[hh, yy] = jnp.where(c == 0, even, odd)
-        sib_out[hh, yy] = jnp.where(c == 0, odd, even).astype(BF16)
-        remote(sib_out.at[hh, yy], sib_in.at[hh, yy], sib_send.at[0], sib_recv.at[it], sib).start()
-
-        @pl.when(it > 0)
-        def _():
-            exchange_first(it - 1)
-
-    exchange_first(jnp.int32(steps - 1))
+        partial_sum(it)
+        send_partial(it)
+        exchange_first(it - LAG)
+
+    pl.loop(steps - LAG, steps)(exchange_first)
 
     wait_recv(cnt_in.at[0], cnt_recv.at[0])
     cnt[1] = cnt[0] + cnt_in[0]
@@ -181,25 +195,6 @@
     pending += [(sib_out, sib_send.at[0]), (cnt.at[0], cnt_send.at[0]), (cnt_in.at[pl.ds(0, NX - 1)], cnt_send.at[1])]
     pending += [(m1x, p1_send.at[0]), (r1x.at[0], p1_send.at[1]), (m1y, p1_send.at[3]), (r1y.at[0], p1_send.at[4])]
     pending += [(r1z.at[pl.ds(0, 5)], p1_send.at[6])]
-
-    @pl.loop(0, steps)
-    def _(it):
-        _, _, hh, yy = place(it)
-        go = 1 + 2 * hh
-        wait_recv(m1x.at[hh, yy], m1x_recv.at[hh, yy])
-        f1x[hh, yy] = (s1[hh, yy, xs(go), :, :, colx].astype(F32) + m1x[hh, yy].astype(F32)).astype(BF16)
-        remote(f1x.at[hh, yy], r1x.at[1, hh, yy], p1_send.at[2], p1x_recv.at[1], dev(xx=xs(go))).start()
-
-    @pl.loop(0, NH)
-    def _(hh):
-        go = 1 + 2 * hh
-        wait_recv(m1y.at[hh], m1y_recv.at[hh])
-
-        @pl.loop(0, NX)
-        def _(xx):
-            f1y[hh, xx] = (s1[hh, ys(go), xx, :, :, coly].astype(F32) + m1y[hh, xx].astype(F32)).astype(BF16)
-
-        remote(f1y.at[hh], r1y.at[1, hh], p1_send.at[5], p1y_recv.at[1], dev(yy=ys(go))).start()
 
     for slot in (2, 3, 4):
         wait_recv(r1z.at[slot], p1z_recv.at[slot])
@@ -212,7 +207,30 @@
             f1z[i, yy] = total.astype(BF16)
         remote(f1z.at[i], r1z.at[5 + i], p1_send.at[7], p1z_recv.at[5 + i], zdev(k)).start()
 
+    @pl.loop(0, steps)
+    def _(it):
+        _, _, hh, yy = place(it)
+        go = 1 + 2 * hh
+        wait_recv(m1x.at[hh, yy], m1x_recv.at[hh, yy])
+        f1x[hh, yy] = (s1[hh, yy, xs(go), :, :, colx].astype(F32) + m1x[hh, yy].astype(F32)).astype(BF16)
+        remote(f1x.at[hh, yy], r1x.at[1, hh, yy], p1_send.at[2], p1x_recv.at[1], dev(xx=xs(go))).start()
+
+    @pl.loop(0, NH)
+    def _(hh):
+        go = 1 + 2 * hh
+        wait_recv(m1y.at[hh], m1y_recv.at[hh])
+
+        @pl.loop(0, NX)
+        def _(xx):
+            f1y[hh, xx] = (s1[hh, ys(go), xx, :, :, coly].astype(F32) + m1y[hh, xx].astype(F32)).astype(BF16)
+
+        remote(f1y.at[hh], r1y.at[1, hh], p1_send.at[5], p1y_recv.at[1], dev(yy=ys(go))).start()
+
     pending += [(f1x, p1_send.at[2]), (f1y, p1_send.at[5]), (f1z, p1_send.at[7])]
+
+    @pl.loop(0, NH * NY * NX)
+    def _(i):
+        nxt_copy(i).start()
 
     for k in range(2):
         wait_recv(r1x.at[k], p1x_recv.at[k])
@@ -316,6 +334,9 @@
     count = count[0:1, 0:1]
 
     pending += [(r3a, p3_send.at[0]), (r3z, p3_send.at[1]), (cnt_in.at[pl.ds(0, NZ - 1)], cnt_send.at[3])]
+
+    for copy in adam_copies:
+        copy.wait()
 
     def adam(cols, summed):
         grad = summed / count
@@ -366,22 +387,36 @@
     pending += [(r3a, a3_send.at[0]), (r3z, a3_send.at[1])]
     pending += [(r2x, a2_send.at[0]), (r2y, a2_send.at[1]), (r2z, a2_send.at[2])]
 
-    for k in yd:
+    def send_x(part, turn):
+        for i in range(2):
+            to = 1 + 2 * i if turn == 0 else 3 - 2 * i
+            gather(w.at[i, part, x, :, c, :, colx], a1_send.at[0], a1x_recv.at[i, turn], dev(xx=xs(to)))
+
+    def send_y(part, turn):
+        for i in range(2):
+            to = 1 + 2 * i if turn == 0 else 3 - 2 * i
+            gather(w.at[i, y, part, :, c, :, coly], a1_send.at[2], a1y_recv.at[i, turn], dev(yy=ys(to)))
+
+    def send_z(part, turn):
+        for i in range(2):
+            to = (2 - turn) * (1 - 2 * i)
+            gather(w.at[h, :, part, l, c, :, colz], a1_send.at[4], a1z_recv.at[2 * turn + i], zdev(to))
+
+    for turn in range(2):
+        send_x(y, turn)
+        send_y(x, turn)
+        send_z(x, turn)
+    for k in (1, 3, 2):
         wait_recv(r2x.at[k - 1], a2x_recv.at[k - 1])
-    for i in range(2):
-        gather(xpart(0, i), a1_send.at[0], a1x_recv.at[i, 0], dev(xx=xs(1 + 2 * i)))
-    for i in range(2):
-        gather(xpart(0, i), a1_send.at[0], a1x_recv.at[i, 1], dev(xx=xs(3 - 2 * i)))
-    for k in xd:
+        send_x(ys(NY - k), 0)
         wait_recv(r2y.at[k - 1], a2y_recv.at[k - 1])
-    for i in range(2):
-        gather(ypart(0, i), a1_send.at[2], a1y_recv.at[i, 0], dev(yy=ys(1 + 2 * i)))
-    for i in range(2):
-        gather(ypart(0, i), a1_send.at[2], a1y_recv.at[i, 1], dev(yy=ys(3 - 2 * i)))
-    for k in xd:
+        send_y(xs(NX - k), 0)
         wait_recv(r2z.at[k - 1], a2z_recv.at[k - 1])
-    for slot, k in enumerate((2, -2, 1, -1)):
-        gather(zpart(0), a1_send.at[4], a1z_recv.at[slot], zdev(k))
+        send_z(xs(NX - k), 0)
+    for k in (1, 3, 2):
+        send_x(ys(NY - k), 1)
+        send_y(xs(NX - k), 1)
+        send_z(xs(NX - k), 1)
     for i in range(2):
         gather(xpart(0, i), f_send.at[0], fx_recv.at[0], sib)
         gather(ypart(0, i), f_send.at[1], fy_recv.at[0], sib)
@@ -462,11 +497,11 @@
     o_proj[:, coly] = acc[:, coly].astype(BF16)
     wait_recv(w.at[:, :, :, :, 1 - c, :, colz], fz_recv.at[0])
 
-    @pl.loop(0, steps)
-    def _(i):
-        hh, yy = lax.div(i, NY), lax.rem(i, NY)
-        lhs = jnp.concatenate([nxt[i * NX + xx] for xx in range(NX)], axis=1)
-        acc[:, colz] += jnp.dot(lhs, w[hh, yy, :, :, :, :, colz].reshape(width, kv - cb), preferred_element_type=F32)
+    @pl.loop(0, NH)
+    def _(hh):
+        lhs = jnp.concatenate([nxt[hh * NY * NX + i] for i in range(NY * NX)], axis=1)
+        rhs = w[hh, :, :, :, :, :, colz].reshape(NY * width, kv - cb)
+        acc[:, colz] += jnp.dot(lhs, rhs, preferred_element_type=F32)
 
     o_proj[:, colz] = acc[:, colz].astype(BF16)
     sec_copy.wait()
@@ -475,20 +510,16 @@
 
 
 def copy_out(*refs):
-    src, dst, held, sem_in, sem_out = refs[:5], refs[5:10], refs[10:15], refs[15], refs[16]
-    parts = []
+    src, dst, sem = refs[:5], refs[5:10], refs[10]
+    copies = []
     for i in range(5):
-        rows = src[i].shape[0]
-        n = PARTS[i]
-        parts += [(i, pl.ds(j * rows // n, rows // n)) for j in range(n)]
-    reads = [pltpu.make_async_copy(src[i].at[r], held[i].at[r], sem_in.at[j]) for j, (i, r) in enumerate(parts)]
-    writes = [pltpu.make_async_copy(held[i].at[r], dst[i].at[r], sem_out.at[j]) for j, (i, r) in enumerate(parts)]
-    for copy in reads:
+        n, rows = PARTS[i], src[i].shape[0]
+        for j in range(n):
+            part = pl.ds(j * rows // n, rows // n)
+            copies.append(pltpu.make_async_copy(src[i].at[part], dst[i].at[part], sem.at[len(copies)]))
+    for copy in copies:
         copy.start()
-    for read, write in zip(reads, writes):
-        read.wait()
-        write.start()
-    for copy in writes:
+    for copy in copies:
         copy.wait()
 
 
@@ -508,6 +539,10 @@
         jax.ShapeDtypeStruct((toks, kv), BF16),
     )
     scratch = [
+        pltpu.SMEM((1,), jnp.int32),
+        pltpu.VMEM((rows, kv), F32),
+        pltpu.VMEM((rows, kv), F32),
+        pltpu.VMEM((rows, kv), F32),
         pltpu.VMEM((NH * NY, toks, width), BF16),
         pltpu.VMEM((toks, kv), BF16),
         pltpu.VMEM((NH * NY * NX, toks, NL * NC * rows), BF16),
@@ -539,7 +574,7 @@
         pltpu.VMEM((toks, kv), F32),
     ]
     sems = (
-        [(1,), (NH * NY,), (NH * NY * NX,), (1,), (1,), (NH * NY,), (4,), (NX + NY + NZ - 2,)]
+        [(5,), (NH * NY,), (NH * NY * NX,), (1,), (1,), (NH * NY,), (4,), (NX + NY + NZ - 2,)]
         + [(8,), (NH, NY), (NH,), (2,), (2,), (7,)]
         + [(3,), (NY - 1,), (NX - 1,), (NX - 1,)]
         + [(2,), (NZ - 1,), (NY - 1,)]
@@ -550,22 +585,22 @@
     )
     results = pl.pallas_call(
         kernel,
-        out_shape=shapes,
-        in_specs=[pl.BlockSpec(memory_space=pltpu.SMEM), anym, anym, anym, vmem, vmem, vmem],
-        out_specs=(vmem, vmem, vmem, anym, vmem),
+        out_shape=[pltpu.VMEM(shape.shape, shape.dtype) for shape in shapes],
+        in_specs=[anym] * 7,
+        out_specs=[vmem] * 5,
         scratch_shapes=scratch + [dma(n) for n in sems],
         compiler_params=pltpu.CompilerParams(
-            collective_id=0, has_side_effects=True, vmem_limit_bytes=58 * 2**20
+            collective_id=0, has_side_effects=True, vmem_limit_bytes=56 * 2**20
         ),
         cost_estimate=pl.CostEstimate(flops=4 * toks * din * kv, bytes_accessed=12 * 2**20, transcendentals=rows * kv),
     )(overflow, tokens, out_grad, next_tokens, master, first_moment, second_moment)
     new_master, new_first, new_second, sec, proj = pl.pallas_call(
         copy_out,
         out_shape=shapes,
-        in_specs=[anym] * 5,
+        in_specs=[vmem] * 5,
         out_specs=[anym] * 5,
-        scratch_shapes=[pltpu.VMEM(shape.shape, shape.dtype) for shape in shapes] + [dma((sum(PARTS),))] * 2,
-        compiler_params=pltpu.CompilerParams(vmem_limit_bytes=58 * 2**20),
+        scratch_shapes=[dma((sum(PARTS),))],
+        compiler_params=pltpu.CompilerParams(vmem_limit_bytes=8 * 2**20),
     )(*results)
     return (new_master, new_first, new_second, sec.reshape(NH * NY * NX, rows, kv), proj)
 

time: 85.5 us -> 80.7 us (0.944)
  Pallas kernels: 84.1 us -> 79.4 us
    pallas_call x2, Pallas kernels: 84.1 us -> 79.4 us  [the longest x1 77.9 us: body(): pl.pallas_call(kernel, out_shape=[pltpu.VMEM(shape.shape, shape.dtype) fo...]
where the time goes in v4:
time: 80.7 us; the launch traced here: 80.6 us
  Pallas kernels  79.4 us (98%)
  between operations  1.29 us (2%)
    pallas_call x1, Pallas kernels, body(): pl.pallas_call(kernel, out_shape=[pltpu.VMEM(shape.shape, shape.dtype) fo...  77.9 us

profile of v4, /device:TPU:1, one launch (start us, length us, event | category | flops | bytes accessed | tf_op | source)
XLA Modules:
  0.0 80.6 jit_solution(11096554295837021442)
XLA Ops:
  1.3 77.9 %shard_map.110 = (f32[16,1024]{1,0:T(8,128)S(1)}, f32[16,1024]{1,0:T(8,128)S(1)}, f32[16,1024]{1,0:T(8,128)S(1)}, bf16[2,4,4,16,1024]{4,3,2,1,0:T(8,128)(2,1)S(1)}, bf16[512,1024]{1,0:T(8,128)(2,1)S(1)}) custom-call(s32[1]{0:T(128)S(6)} %copy.12.ov_hbm, bf16[512,4096]{1,0:T(8,128)(2,1)} %tok_hbm.1, bf16[512,1024]{1,0:T(8,128)(2,1)} %og_hbm.1, ...), custom_call_target="tpu_custom_call" | custom-call | flops 8589934592 | bytes 12582912 | tf_op jit(solution)/shard_map/pallas_call | solution.py:586
  79.2 1.4 %shard_map.111 = (f32[16,1024]{1,0:T(8,128)}, f32[16,1024]{1,0:T(8,128)}, f32[16,1024]{1,0:T(8,128)}, bf16[2,4,4,16,1024]{4,3,2,1,0:T(8,128)(2,1)}, bf16[512,1024]{1,0:T(8,128)(2,1)}) custom-call(f32[16,1024]{1,0:T(8,128)S(1)} %get-tuple-element.15.refs_0_, f32[16,1024]{1,0:T(8,128)S(1)} %get-tuple-element.16.refs_1_, ...), custom_call_target="tpu_custom_call" | custom-call | tf_op jit(solution)/shard_map/pallas_call | solution.py:597

commit v5 on v4

--- a/solution.py
+++ b/solution.py
@@ -97,8 +97,8 @@
         pltpu.make_async_copy(src, dst, in_sem.at[2 + i])
         for i, (src, dst) in enumerate(((master_hbm, master), (first_hbm, first), (second_hbm, second)))
     ]
+    ov_copy.start()
     og_copy.start()
-    ov_copy.start()
     width = NX * NL * NC * rows
     steps = NH * NY
 
@@ -111,13 +111,12 @@
         cols = pl.ds(pl.multiple_of((hh * NY + yy) * width, width), width)
         return pltpu.make_async_copy(tok_hbm.at[:, cols], tok.at[it], tok_sem.at[it])
 
-    @pl.loop(0, steps)
-    def _(it):
+    def start_tok(it):
         tok_copy(it).start()
 
-    for copy in adam_copies:
-        copy.start()
+    pl.loop(0, LAG)(start_tok)
     og_copy.wait()
+    pl.loop(LAG, steps)(start_tok)
     ov_copy.wait()
     kept = (1 - ov[0]).astype(F32)
     og[...] = og[...] * kept.astype(BF16)
@@ -196,6 +195,26 @@
     pending += [(m1x, p1_send.at[0]), (r1x.at[0], p1_send.at[1]), (m1y, p1_send.at[3]), (r1y.at[0], p1_send.at[4])]
     pending += [(r1z.at[pl.ds(0, 5)], p1_send.at[6])]
 
+    def relay_x(it):
+        _, _, hh, yy = place(it)
+        go = 1 + 2 * hh
+        wait_recv(m1x.at[hh, yy], m1x_recv.at[hh, yy])
+        f1x[hh, yy] = (s1[hh, yy, xs(go), :, :, colx].astype(F32) + m1x[hh, yy].astype(F32)).astype(BF16)
+        remote(f1x.at[hh, yy], r1x.at[1, hh, yy], p1_send.at[2], p1x_recv.at[1], dev(xx=xs(go))).start()
+
+    @pl.loop(0, NH)
+    def _(hh):
+        go = 1 + 2 * hh
+        wait_recv(m1y.at[hh], m1y_recv.at[hh])
+
+        @pl.loop(0, NX)
+        def _(xx):
+            f1y[hh, xx] = (s1[hh, ys(go), xx, :, :, coly].astype(F32) + m1y[hh, xx].astype(F32)).astype(BF16)
+
+        remote(f1y.at[hh], r1y.at[1, hh], p1_send.at[5], p1y_recv.at[1], dev(yy=ys(go))).start()
+
+    pl.loop(0, steps - LAG)(relay_x)
+
     for slot in (2, 3, 4):
         wait_recv(r1z.at[slot], p1z_recv.at[slot])
     for i, k in ((0, 2), (1, NZ - 2)):
@@ -207,30 +226,16 @@
             f1z[i, yy] = total.astype(BF16)
         remote(f1z.at[i], r1z.at[5 + i], p1_send.at[7], p1z_recv.at[5 + i], zdev(k)).start()
 
-    @pl.loop(0, steps)
-    def _(it):
-        _, _, hh, yy = place(it)
-        go = 1 + 2 * hh
-        wait_recv(m1x.at[hh, yy], m1x_recv.at[hh, yy])
-        f1x[hh, yy] = (s1[hh, yy, xs(go), :, :, colx].astype(F32) + m1x[hh, yy].astype(F32)).astype(BF16)
-        remote(f1x.at[hh, yy], r1x.at[1, hh, yy], p1_send.at[2], p1x_recv.at[1], dev(xx=xs(go))).start()
-
-    @pl.loop(0, NH)
-    def _(hh):
-        go = 1 + 2 * hh
-        wait_recv(m1y.at[hh], m1y_recv.at[hh])
-
-        @pl.loop(0, NX)
-        def _(xx):
-            f1y[hh, xx] = (s1[hh, ys(go), xx, :, :, coly].astype(F32) + m1y[hh, xx].astype(F32)).astype(BF16)
-
-        remote(f1y.at[hh], r1y.at[1, hh], p1_send.at[5], p1y_recv.at[1], dev(yy=ys(go))).start()
+    pl.loop(steps - LAG, steps)(relay_x)
 
     pending += [(f1x, p1_send.at[2]), (f1y, p1_send.at[5]), (f1z, p1_send.at[7])]
 
     @pl.loop(0, NH * NY * NX)
     def _(i):
         nxt_copy(i).start()
+
+    for copy in adam_copies:
+        copy.start()
 
     for k in range(2):
         wait_recv(r1x.at[k], p1x_recv.at[k])

time: 80.7 us -> 78.5 us (0.973)
  Pallas kernels: 79.4 us -> 77.1 us
    pallas_call x1, Pallas kernels: 77.9 us -> 75.7 us  [body(): pl.pallas_call(kernel, out_shape=[pltpu.VMEM(shape.shape, shape.dtype) fo...]
where the time goes in v5:
time: 78.5 us; the launch traced here: 78.4 us
  Pallas kernels  77.1 us (98%)
  between operations  1.29 us (2%)
    pallas_call x1, Pallas kernels, body(): pl.pallas_call(kernel, out_shape=[pltpu.VMEM(shape.shape, shape.dtype) fo...  75.7 us

profile of v5, /device:TPU:1, one launch (start us, length us, event | category | flops | bytes accessed | tf_op | source)
XLA Modules:
  0.0 78.4 jit_solution(10934856551501805853)
XLA Ops:
  1.3 75.7 %shard_map.110 = (f32[16,1024]{1,0:T(8,128)S(1)}, f32[16,1024]{1,0:T(8,128)S(1)}, f32[16,1024]{1,0:T(8,128)S(1)}, bf16[2,4,4,16,1024]{4,3,2,1,0:T(8,128)(2,1)S(1)}, bf16[512,1024]{1,0:T(8,128)(2,1)S(1)}) custom-call(s32[1]{0:T(128)S(6)} %copy.12.ov_hbm, bf16[512,4096]{1,0:T(8,128)(2,1)} %tok_hbm.1, bf16[512,1024]{1,0:T(8,128)(2,1)} %og_hbm.1, ...), custom_call_target="tpu_custom_call" | custom-call | flops 8589934592 | bytes 12582912 | tf_op jit(solution)/shard_map/pallas_call | solution.py:591
  77.0 1.4 %shard_map.111 = (f32[16,1024]{1,0:T(8,128)}, f32[16,1024]{1,0:T(8,128)}, f32[16,1024]{1,0:T(8,128)}, bf16[2,4,4,16,1024]{4,3,2,1,0:T(8,128)(2,1)}, bf16[512,1024]{1,0:T(8,128)(2,1)}) custom-call(f32[16,1024]{1,0:T(8,128)S(1)} %get-tuple-element.15.refs_0_, f32[16,1024]{1,0:T(8,128)S(1)} %get-tuple-element.16.refs_1_, ...), custom_call_target="tpu_custom_call" | custom-call | tf_op jit(solution)/shard_map/pallas_call | solution.py:602

commit v6 on v5

--- a/solution.py
+++ b/solution.py
@@ -58,8 +58,8 @@
         zz = lax.rem(h * NL + l + k + NZ, NZ)
         return lax.div(zz, NL), lax.rem(zz, NL)
 
-    xd, yd = range(1, NX), range(1, NY)
-    zd = [(e, f) for e in range(NH) for f in range(NL)][1:]
+    xd = yd = (2, 1, 3)
+    zd = [(1, f) for f in range(NL)] + [(0, f) for f in range(1, NL)]
     sib = dev(cc=1 - c)
 
     def remote(src, dst, send, recv, to):
@@ -360,20 +360,20 @@
     def gather(ref, send, recv, to):
         remote(ref, ref, send, recv, to).start()
 
+    for k in yd:
+        gather(w.at[h, y, x, l, c, :, colz], a3_send.at[1], a3z_recv.at[k - 1], dev(yy=ys(k)))
     for e, f in zd:
         gather(w.at[h, y, x, l, c, :, colxy], a3_send.at[0], a3a_recv.at[e * NL + f - 1], dev(hh=hs(e), ll=ls(f)))
     for k in yd:
-        gather(w.at[h, y, x, l, c, :, colz], a3_send.at[1], a3z_recv.at[k - 1], dev(yy=ys(k)))
+        wait_recv(r3z.at[k - 1], a3z_recv.at[k - 1])
+    for k in xd:
+        gather(w.at[h, :, x, l, c, :, colz], a2_send.at[2], a2z_recv.at[k - 1], dev(xx=xs(k)))
     for k in range(1, NZ):
         wait_recv(r3a.at[k - 1], a3a_recv.at[k - 1])
     for k in yd:
         gather(w.at[:, y, x, :, c, :, colx], a2_send.at[0], a2x_recv.at[k - 1], dev(yy=ys(k)))
     for k in xd:
         gather(w.at[:, y, x, :, c, :, coly], a2_send.at[1], a2y_recv.at[k - 1], dev(xx=xs(k)))
-    for k in yd:
-        wait_recv(r3z.at[k - 1], a3z_recv.at[k - 1])
-    for k in xd:
-        gather(w.at[h, :, x, l, c, :, colz], a2_send.at[2], a2z_recv.at[k - 1], dev(xx=xs(k)))
 
     def xpart(k, hh):
         return w.at[hh, :, xs(k), :, c, :, colx]
@@ -405,19 +405,20 @@
     def send_z(part, turn):
         for i in range(2):
             to = (2 - turn) * (1 - 2 * i)
-            gather(w.at[h, :, part, l, c, :, colz], a1_send.at[4], a1z_recv.at[2 * turn + i], zdev(to))
+            gather(w.at[h, :, part, l, c, :, colz], a1_send.at[4], a1z_recv.at[2 * turn + i, part], zdev(to))
 
     for turn in range(2):
         send_x(y, turn)
         send_y(x, turn)
         send_z(x, turn)
     for k in (1, 3, 2):
+        wait_recv(r2z.at[k - 1], a2z_recv.at[k - 1])
+        send_z(xs(NX - k), 0)
+    for k in (1, 3, 2):
         wait_recv(r2x.at[k - 1], a2x_recv.at[k - 1])
         send_x(ys(NY - k), 0)
         wait_recv(r2y.at[k - 1], a2y_recv.at[k - 1])
         send_y(xs(NX - k), 0)
-        wait_recv(r2z.at[k - 1], a2z_recv.at[k - 1])
-        send_z(xs(NX - k), 0)
     for k in (1, 3, 2):
         send_x(ys(NY - k), 1)
         send_y(xs(NX - k), 1)
@@ -427,15 +428,23 @@
         gather(ypart(0, i), f_send.at[1], fy_recv.at[0], sib)
     gather(zpart(0), f_send.at[2], fz_recv.at[0], sib)
 
+    def relay_z(part):
+        for i, k in enumerate((-2, 2)):
+            wait_recv(r1z.at[0, :, 0], a1z_recv.at[i, part])
+            hh, ll = zat(k)
+            gather(w.at[hh, :, part, ll, c, :, colz], a1_send.at[5], a1z_recv.at[6 + i, 0], zdev(-k // 2))
+            half = pl.ds(i * (NY // 2), NY // 2)
+            gather(w.at[hh, half, part, ll, c, :, colz], a1_send.at[5], a1z_recv.at[4 + i, 0], zdev(-k))
+
+    relay_z(x)
+    relay_z(xs(NX - 1))
+    relay_z(xs(NX - 3))
+    relay_z(xs(NX - 2))
     for i in range(2):
         wait_recv(m1x.at[0], a1x_recv.at[i, 0])
         gather(xpart(3 - 2 * i, i), a1_send.at[1], a1x_recv.at[i, 2], dev(xx=xs(1 + 2 * i)))
         wait_recv(m1y.at[0], a1y_recv.at[i, 0])
         gather(ypart(3 - 2 * i, i), a1_send.at[3], a1y_recv.at[i, 2], dev(yy=ys(1 + 2 * i)))
-    for i, k in enumerate((-2, 2)):
-        wait_recv(r1z.at[0], a1z_recv.at[i])
-        gather(zhalf(k, i), a1_send.at[5], a1z_recv.at[4 + i], zdev(-k))
-        gather(zpart(k), a1_send.at[5], a1z_recv.at[6 + i], zdev(-k // 2))
     for i in range(2):
         gather(xpart(3 - 2 * i, i), f_send.at[0], fx_recv.at[3 - 2 * i], sib)
         gather(ypart(3 - 2 * i, i), f_send.at[1], fy_recv.at[3 - 2 * i], sib)
@@ -474,7 +483,8 @@
     wait_recv(r1y.at[0], fy_recv.at[0])
     project_y(0)
     for i, k in enumerate((-1, 1)):
-        wait_recv(r1z.at[0], a1z_recv.at[2 + i])
+        for part in range(NX):
+            wait_recv(r1z.at[0, :, 0], a1z_recv.at[2 + i, part])
         gather(zpart(k), f_send.at[2], fz_recv.at[0], sib)
     for k in (1, 3):
         wait_recv(r1x.at[0], fx_recv.at[k])
@@ -487,10 +497,10 @@
         wait_recv(m1y.at[0], a1y_recv.at[i, 2])
         gather(ypart(2, i), f_send.at[1], fy_recv.at[2], sib)
     for i, k in enumerate((-3, 3)):
-        wait_recv(r1z.at[0], a1z_recv.at[6 + i])
+        wait_recv(r1z.at[0], a1z_recv.at[6 + i, 0])
         gather(zpart(k), f_send.at[2], fz_recv.at[0], sib)
     for i in range(2):
-        wait_recv(r1z.at[0, pl.ds(0, NY // 2)], a1z_recv.at[4 + i])
+        wait_recv(r1z.at[0, pl.ds(0, NY // 2)], a1z_recv.at[4 + i, 0])
         gather(zhalf(4, i), f_send.at[2], fz_recv.at[0], sib)
     sec_copy = pltpu.make_async_copy(w.at[:, :, :, l, c], o_sec, out_sem.at[0])
     sec_copy.start()
@@ -585,7 +595,7 @@
         + [(2,), (NZ - 1,), (NY - 1,)]
         + [(2,), (NZ - 1,), (NY - 1,)]
         + [(3,), (NY - 1,), (NX - 1,), (NX - 1,)]
-        + [(6,), (2, 3), (2, 3), (8,)]
+        + [(6,), (2, 3), (2, 3), (8, NX)]
         + [(3,), (NX,), (NY,), (1,)]
     )
     results = pl.pallas_call(

time: 78.5 us -> 77.6 us (0.989)
  Pallas kernels: 77.1 us -> 76.2 us
    pallas_call x1, Pallas kernels: 75.7 us -> 74.8 us  [body(): pl.pallas_call(kernel, out_shape=[pltpu.VMEM(shape.shape, shape.dtype) fo...]
where the time goes in v6:
time: 77.6 us; the launch traced here: 77.5 us
  Pallas kernels  76.2 us (98%)
  between operations  1.29 us (2%)
    pallas_call x1, Pallas kernels, body(): pl.pallas_call(kernel, out_shape=[pltpu.VMEM(shape.shape, shape.dtype) fo...  74.8 us

profile of v6, /device:TPU:1, one launch (start us, length us, event | category | flops | bytes accessed | tf_op | source)
XLA Modules:
  0.0 77.5 jit_solution(3143583781372187405)
XLA Ops:
  1.3 74.8 %shard_map.110 = (f32[16,1024]{1,0:T(8,128)S(1)}, f32[16,1024]{1,0:T(8,128)S(1)}, f32[16,1024]{1,0:T(8,128)S(1)}, bf16[2,4,4,16,1024]{4,3,2,1,0:T(8,128)(2,1)S(1)}, bf16[512,1024]{1,0:T(8,128)(2,1)S(1)}) custom-call(s32[1]{0:T(128)S(6)} %copy.12.ov_hbm, bf16[512,4096]{1,0:T(8,128)(2,1)} %tok_hbm.1, bf16[512,1024]{1,0:T(8,128)(2,1)} %og_hbm.1, ...), custom_call_target="tpu_custom_call" | custom-call | flops 8589934592 | bytes 12582912 | tf_op jit(solution)/shard_map/pallas_call | solution.py:601
  76.0 1.4 %shard_map.111 = (f32[16,1024]{1,0:T(8,128)}, f32[16,1024]{1,0:T(8,128)}, f32[16,1024]{1,0:T(8,128)}, bf16[2,4,4,16,1024]{4,3,2,1,0:T(8,128)(2,1)}, bf16[512,1024]{1,0:T(8,128)(2,1)}) custom-call(f32[16,1024]{1,0:T(8,128)S(1)} %get-tuple-element.15.refs_0_, f32[16,1024]{1,0:T(8,128)S(1)} %get-tuple-element.16.refs_1_, ...), custom_call_target="tpu_custom_call" | custom-call | tf_op jit(solution)/shard_map/pallas_call | solution.py:612

commit v7 on v6

--- a/solution.py
+++ b/solution.py
@@ -228,6 +228,12 @@
 
     pl.loop(steps - LAG, steps)(relay_x)
 
+    for k in xd:
+        wait_recv(cnt_in.at[k], cnt_recv.at[k])
+    cnt[2] = cnt[1] + cnt_in[1] + cnt_in[2] + cnt_in[3]
+    for k in yd:
+        remote(cnt.at[2], cnt_in.at[NX - 1 + k], cnt_send.at[2], cnt_recv.at[NX - 1 + k], dev(yy=ys(k))).start()
+
     pending += [(f1x, p1_send.at[2]), (f1y, p1_send.at[5]), (f1z, p1_send.at[7])]
 
     @pl.loop(0, NH * NY * NX)
@@ -278,11 +284,13 @@
     for k in xd:
         remote(s2z.at[:, xs(k)], r2z.at[k - 1], p2_send.at[2], p2z_recv.at[k - 1], dev(xx=xs(k))).start()
 
-    for k in xd:
-        wait_recv(cnt_in.at[k], cnt_recv.at[k])
-    cnt[2] = cnt[1] + cnt_in[1] + cnt_in[2] + cnt_in[3]
-    for k in yd:
-        remote(cnt.at[2], cnt_in.at[NX - 1 + k], cnt_send.at[2], cnt_recv.at[NX - 1 + k], dev(yy=ys(k))).start()
+    base = NX + NY - 1
+    for k in yd:
+        wait_recv(cnt_in.at[NX - 1 + k], cnt_recv.at[NX - 1 + k])
+    cnt[3] = cnt[2] + cnt_in[NX] + cnt_in[NX + 1] + cnt_in[NX + 2]
+    for e, f in zd:
+        slot = base + e * NL + f - 1
+        remote(cnt.at[3], cnt_in.at[slot], cnt_send.at[3], cnt_recv.at[slot], dev(hh=hs(e), ll=ls(f))).start()
 
     pending += [(r2x, p2_send.at[0]), (r2y, p2_send.at[1]), (r2z, p2_send.at[2])]
     pending += [(cnt_in.at[pl.ds(0, NY - 1)], cnt_send.at[2])]
@@ -313,24 +321,11 @@
     for k in yd:
         remote(s3z.at[ys(k)], r3z.at[k - 1], p3_send.at[1], p3z_recv.at[k - 1], dev(yy=ys(k))).start()
 
-    base = NX + NY - 1
-    for k in yd:
-        wait_recv(cnt_in.at[NX - 1 + k], cnt_recv.at[NX - 1 + k])
-    cnt[3] = cnt[2] + cnt_in[NX] + cnt_in[NX + 1] + cnt_in[NX + 2]
-    for e, f in zd:
-        slot = base + e * NL + f - 1
-        remote(cnt.at[3], cnt_in.at[slot], cnt_send.at[3], cnt_recv.at[slot], dev(hh=hs(e), ll=ls(f))).start()
-
     for k in range(1, NZ):
         wait_recv(r3a.at[k - 1], p3a_recv.at[k - 1])
     sum_a = s3a[h, l].astype(F32)
     for k in range(1, NZ):
         sum_a += r3a[k - 1].astype(F32)
-    for k in yd:
-        wait_recv(r3z.at[k - 1], p3z_recv.at[k - 1])
-    sum_z = s3z[y].astype(F32)
-    for k in yd:
-        sum_z += r3z[k - 1].astype(F32)
     for k in range(1, NZ):
         wait_recv(cnt_in.at[base + k - 1], cnt_recv.at[base + k - 1])
     count = cnt[3]
@@ -355,15 +350,20 @@
         w[h, y, x, l, c, :, cols] = new_master.astype(BF16)
 
     adam(colxy, sum_a)
-    adam(colz, sum_z)
 
     def gather(ref, send, recv, to):
         remote(ref, ref, send, recv, to).start()
 
-    for k in yd:
-        gather(w.at[h, y, x, l, c, :, colz], a3_send.at[1], a3z_recv.at[k - 1], dev(yy=ys(k)))
     for e, f in zd:
         gather(w.at[h, y, x, l, c, :, colxy], a3_send.at[0], a3a_recv.at[e * NL + f - 1], dev(hh=hs(e), ll=ls(f)))
+    for k in yd:
+        wait_recv(r3z.at[k - 1], p3z_recv.at[k - 1])
+    sum_z = s3z[y].astype(F32)
+    for k in yd:
+        sum_z += r3z[k - 1].astype(F32)
+    adam(colz, sum_z)
+    for k in yd:
+        gather(w.at[h, y, x, l, c, :, colz], a3_send.at[1], a3z_recv.at[k - 1], dev(yy=ys(k)))
     for k in yd:
         wait_recv(r3z.at[k - 1], a3z_recv.at[k - 1])
     for k in xd:

time: 77.6 us -> 76.2 us (0.982)
  Pallas kernels: 76.2 us -> 74.8 us
    pallas_call x1, Pallas kernels: 74.8 us -> 73.4 us  [body(): pl.pallas_call(kernel, out_shape=[pltpu.VMEM(shape.shape, shape.dtype) fo...]
where the time goes in v7:
time: 76.2 us; the launch traced here: 76.1 us
  Pallas kernels  74.8 us (98%)
  between operations  1.29 us (2%)
    pallas_call x1, Pallas kernels, body(): pl.pallas_call(kernel, out_shape=[pltpu.VMEM(shape.shape, shape.dtype) fo...  73.4 us

profile of v7, /device:TPU:1, one launch (start us, length us, event | category | flops | bytes accessed | tf_op | source)
XLA Modules:
  0.0 76.1 jit_solution(13360778514041817303)
XLA Ops:
  1.3 73.4 %shard_map.110 = (f32[16,1024]{1,0:T(8,128)S(1)}, f32[16,1024]{1,0:T(8,128)S(1)}, f32[16,1024]{1,0:T(8,128)S(1)}, bf16[2,4,4,16,1024]{4,3,2,1,0:T(8,128)(2,1)S(1)}, bf16[512,1024]{1,0:T(8,128)(2,1)S(1)}) custom-call(s32[1]{0:T(128)S(6)} %copy.12.ov_hbm, bf16[512,4096]{1,0:T(8,128)(2,1)} %tok_hbm.1, bf16[512,1024]{1,0:T(8,128)(2,1)} %og_hbm.1, ...), custom_call_target="tpu_custom_call" | custom-call | flops 8589934592 | bytes 12582912 | tf_op jit(solution)/shard_map/pallas_call | solution.py:601
  74.6 1.4 %shard_map.111 = (f32[16,1024]{1,0:T(8,128)}, f32[16,1024]{1,0:T(8,128)}, f32[16,1024]{1,0:T(8,128)}, bf16[2,4,4,16,1024]{4,3,2,1,0:T(8,128)(2,1)}, bf16[512,1024]{1,0:T(8,128)(2,1)}) custom-call(f32[16,1024]{1,0:T(8,128)S(1)} %get-tuple-element.15.refs_0_, f32[16,1024]{1,0:T(8,128)S(1)} %get-tuple-element.16.refs_1_, ...), custom_call_target="tpu_custom_call" | custom-call | tf_op jit(solution)/shard_map/pallas_call | solution.py:612

commit v8 on v7

--- a/solution.py
+++ b/solution.py
@@ -295,23 +295,28 @@
     pending += [(r2x, p2_send.at[0]), (r2y, p2_send.at[1]), (r2z, p2_send.at[2])]
     pending += [(cnt_in.at[pl.ds(0, NY - 1)], cnt_send.at[2])]
 
+    def send_sums(cols):
+        for e, f in zd:
+            slot = e * NL + f - 1
+            remote(
+                s3a.at[hs(e), ls(f), :, cols], r3a.at[slot, :, cols], p3_send.at[0], p3a_recv.at[slot],
+                dev(hh=hs(e), ll=ls(f)),
+            ).start()
+
     for k in yd:
         wait_recv(r2x.at[k - 1], p2x_recv.at[k - 1])
     total = s2x[:, y].astype(F32)
     for k in yd:
         total += r2x[k - 1].astype(F32)
     s3a[:, :, :, colx] = total.astype(BF16)
+    send_sums(colx)
     for k in xd:
         wait_recv(r2y.at[k - 1], p2y_recv.at[k - 1])
     total = s2y[:, x].astype(F32)
     for k in xd:
         total += r2y[k - 1].astype(F32)
     s3a[:, :, :, coly] = total.astype(BF16)
-    for e, f in zd:
-        slot = e * NL + f - 1
-        remote(
-            s3a.at[hs(e), ls(f)], r3a.at[slot], p3_send.at[0], p3a_recv.at[slot], dev(hh=hs(e), ll=ls(f))
-        ).start()
+    send_sums(coly)
     for k in xd:
         wait_recv(r2z.at[k - 1], p2z_recv.at[k - 1])
     total = s2z[:, x].astype(F32)

time: 76.2 us -> 74.9 us (0.983)
  Pallas kernels: 74.8 us -> 73.5 us
    pallas_call x1, Pallas kernels: 73.4 us -> 72.1 us  [body(): pl.pallas_call(kernel, out_shape=[pltpu.VMEM(shape.shape, shape.dtype) fo...]
where the time goes in v8:
time: 74.9 us; the launch traced here: 74.8 us
  Pallas kernels  73.5 us (98%)
  between operations  1.29 us (2%)
    pallas_call x1, Pallas kernels, body(): pl.pallas_call(kernel, out_shape=[pltpu.VMEM(shape.shape, shape.dtype) fo...  72.1 us

profile of v8, /device:TPU:1, one launch (start us, length us, event | category | flops | bytes accessed | tf_op | source)
XLA Modules:
  0.0 74.8 jit_solution(15963606392977790320)
XLA Ops:
  1.3 72.1 %shard_map.110 = (f32[16,1024]{1,0:T(8,128)S(1)}, f32[16,1024]{1,0:T(8,128)S(1)}, f32[16,1024]{1,0:T(8,128)S(1)}, bf16[2,4,4,16,1024]{4,3,2,1,0:T(8,128)(2,1)S(1)}, bf16[512,1024]{1,0:T(8,128)(2,1)S(1)}) custom-call(s32[1]{0:T(128)S(6)} %copy.12.ov_hbm, bf16[512,4096]{1,0:T(8,128)(2,1)} %tok_hbm.1, bf16[512,1024]{1,0:T(8,128)(2,1)} %og_hbm.1, ...), custom_call_target="tpu_custom_call" | custom-call | flops 8589934592 | bytes 12582912 | tf_op jit(solution)/shard_map/pallas_call | solution.py:606
  73.4 1.4 %shard_map.111 = (f32[16,1024]{1,0:T(8,128)}, f32[16,1024]{1,0:T(8,128)}, f32[16,1024]{1,0:T(8,128)}, bf16[2,4,4,16,1024]{4,3,2,1,0:T(8,128)(2,1)}, bf16[512,1024]{1,0:T(8,128)(2,1)}) custom-call(f32[16,1024]{1,0:T(8,128)S(1)} %get-tuple-element.15.refs_0_, f32[16,1024]{1,0:T(8,128)S(1)} %get-tuple-element.16.refs_1_, ...), custom_call_target="tpu_custom_call" | custom-call | tf_op jit(solution)/shard_map/pallas_call | solution.py:617
